TPU v7x, 512 devices: a whole 4x4x16 slice. The times are simulated.
512 devices in a mesh: band: 32 (over z, y_lo), grid: 16 (over x, y_hi, core).
Axes of the slice: x: 4, y: 4 (y_hi: 2, y_lo: 2; y = y_hi * 2 + y_lo), z: 16, core: 2. Of those that a mesh axis runs over, the one named last changes fastest.
Arguments:
- orbitals: float32 [64, 96, 96, 128], P('band', 'grid'), may hold values from -6 to 6
- kernel: float32 [96, 96, 128], P(None, 'grid'), as said below
- owners: int32 [1], replicated, may hold values from 0 to 31
Outputs:
- exchange_applied: float32 [64, 96, 96, 128], P('band', 'grid')
Inputs may be any that keep to these rules, and one draw needn't show every extreme that they name: kernel is zero at the zero frequency, positive elsewhere, and even: its value at indices (a, b, c) equals that at ((-a) mod 96, (-b) mod 96, (-c) mod 128).
All inputs are finite; a program needn't handle non-finite values.
Results may differ from a plain program's by a relative error of at most 0.0003.
Values sent between devices are 32-bit elements; how exact they have to be, the bound alone decides.
No kernel may reach another device: no remote copies, remote signals or barrier semaphores. Data moves between devices by JAX's collectives and lax.ppermute only.
A program may use at most 64 MiB of HBM per device.

v0:
```python
import math

import jax
import jax.numpy as jnp
from jax import lax
from jax.sharding import PartitionSpec as P

precise = lax.Precision.HIGHEST
mixing = 0.25


def broadcast(block, axis, holder):
    block = jnp.where(lax.axis_index(axis) == holder, block, jnp.zeros_like(block))
    return lax.psum(block, axis)


def twiddle(length):
    counter = jnp.arange(length, dtype=jnp.int32)
    phases = counter[:, None] * counter[None, :] % length
    angles = phases.astype(jnp.float32) * (2.0 * math.pi / length)
    return (jnp.cos(angles), jnp.sin(angles))


def along_dim(spectrum, cosine, sine_part, letters, forward):
    with_cosine = jnp.einsum(
        letters, cosine, spectrum, precision=precise, preferred_element_type=jnp.float32
    )
    with_sine = jnp.einsum(
        letters, sine_part, spectrum, precision=precise, preferred_element_type=jnp.float32
    )
    middle = spectrum.shape[-1] // 2
    real_cosine, imag_cosine = (with_cosine[..., :middle], with_cosine[..., middle:])
    real_sine, imag_sine = (with_sine[..., :middle], with_sine[..., middle:])
    if forward:
        return jnp.concatenate([real_cosine + imag_sine, imag_cosine - real_sine], axis=-1)
    return jnp.concatenate([real_cosine - imag_sine, imag_cosine + real_sine], axis=-1)


def local(orbitals, kernel, owners):
    orb_count, slab_x, rows_y, cells_z = orbitals.shape
    full_x = slab_x * lax.axis_size("grid")
    cosine_x, sine_x = twiddle(full_x)
    cosine_y, sine_y = twiddle(rows_y)
    cosine_z, sine_z = twiddle(cells_z)
    norm_scale = 1.0 / (full_x * rows_y * cells_z)
    kernel_pair = jnp.concatenate([kernel, kernel], axis=-1)
    forward_z = jnp.concatenate([cosine_z, -sine_z], axis=1)
    inverse_z = jnp.concatenate([cosine_z, -sine_z], axis=0) * norm_scale
    pair_count = orb_count * orb_count
    source_block = broadcast(orbitals, "band", owners[0])
    density = (orbitals[:, None] * source_block[None, :]).reshape(
        pair_count, slab_x, rows_y, cells_z
    )
    spectrum = jnp.dot(density, forward_z, precision=precise, preferred_element_type=jnp.float32)
    spectrum = along_dim(spectrum, cosine_y, sine_y, "ky,bxyc->bxkc", True)
    columns = lax.all_to_all(spectrum, "grid", split_axis=2, concat_axis=1, tiled=True)
    spectral_spectrum = along_dim(columns, cosine_x, sine_x, "kx,bxyc->bkyc", True)
    spectral_spectrum = spectral_spectrum * kernel_pair
    spectral_spectrum = along_dim(spectral_spectrum, cosine_x, sine_x, "kx,bxyc->bkyc", False)
    spectrum = lax.all_to_all(spectral_spectrum, "grid", split_axis=1, concat_axis=2, tiled=True)
    spectrum = along_dim(spectrum, cosine_y, sine_y, "ky,bxyc->bxkc", False)
    potential = jnp.dot(spectrum, inverse_z, precision=precise, preferred_element_type=jnp.float32)
    potential = potential.reshape(orb_count, orb_count, slab_x, rows_y, cells_z)
    accumulated = jnp.sum(source_block[None] * potential, axis=1)
    return -mixing * accumulated


def solution(mesh):
    return jax.shard_map(
        local,
        mesh=mesh,
        in_specs=(P("band", "grid", None, None), P(None, "grid", None), P()),
        out_specs=P("band", "grid", None, None),
        check_vma=False,
    )
```

profile of v0, /device:TPU:1, one launch (start us, length us, event | category | flops | bytes accessed | tf_op | source)
XLA Modules:
  0.0 396.4 jit_solution(17879300275134123675)
XLA Ops:
  6.5 0.0 all-reduce.2.cloned.1.call-start
  7.2 0.9 broadcast_select_fusion
  8.1 0.0 all-reduce.2.cloned.1.call-update
  8.1 0.3 sine_negate_fusion
  8.4 247.2 %all-reduce.2.cloned.1.call-done = f32[2,6,96,128]{3,2,1,0:T(8,128)} async-done(((f32[2,6,96,128]{3,2,1,0:T(8,128)}), f32[2,6,96,128]{3,2,1,0:T(8,128)}) %all-reduce.2.cloned.1.call-update) | async-done | bytes 589840 | tf_op jit(solution)/shard_map/psum | solution.py:14
  255.6 1.4 broadcast_multiply_fusion
  257.0 2.0 fusion.30
  259.0 2.5 convolution_bitcast_fusion
  261.5 2.4 convolution_bitcast_fusion.1
  263.9 0.3 slice_add_fusion.3
  264.2 0.2 pad_maximum_fusion
  264.4 2.9 copy.24
  267.3 29.5 %all-to-all-start = ((f32[4,6,96,256]{3,0,1,2:T(4,128)}), f32[4,6,96,256]{3,0,1,2:T(4,128)S(1)}, u32[]{:S(2)}, u32[]{:S(2)}) async-start(f32[4,6,96,256]{3,0,1,2:T(4,128)} %copy.24), calls=%async_computation | async-start | bytes 4718592 | tf_op jit(solution)/shard_map/all_to_all | solution.py:56
  296.8 0.0 copy-done.1
  296.9 31.2 %all-to-all-done = f32[4,6,96,256]{3,0,1,2:T(4,128)S(1)} async-done(((f32[4,6,96,256]{3,0,1,2:T(4,128)}), f32[4,6,96,256]{3,0,1,2:T(4,128)S(1)}, u32[]{:S(2)}, u32[]{:S(2)}) %all-to-all-start) | async-done | bytes 2359328 | tf_op jit(solution)/shard_map/all_to_all | solution.py:56
  328.1 0.4 copy.26
  328.5 3.0 fusion.16
  331.5 3.1 fusion.19
  334.6 0.3 slice_add_fusion.2
  334.9 2.6 fusion.14
  337.5 2.6 fusion.15
  340.1 0.3 slice_subtract_fusion.1
  340.4 0.4 pad_maximum_fusion.1
  340.8 1.5 copy.29
  342.3 37.5 %all_to_all.36 = f32[4,96,6,256]{3,0,2,1:T(4,128)S(1)} all-to-all(f32[4,96,6,256]{3,0,2,1:T(4,128)S(1)} %copy.29), channel_id=1, replica_groups=mesh['band'=32,'grid'=16] {'grid'}, dimensions={1} | all-to-all | bytes 4718592 | tf_op jit(solution)/shard_map/all_to_all | solution.py:60
  379.8 0.5 copy.30
  380.3 2.6 fusion.22
  383.0 2.6 fusion.25
  385.6 0.3 slice_subtract_fusion
  385.9 0.7 copy-done
  386.7 2.0 multiply_reduce_fusion
  388.7 0.9 broadcast_multiply_fusion.1
  (3 shorter events, 0.0 us)
Async XLA Ops:
  6.5 249.1 %all-reduce.2.cloned.1.call-start = ((), (), s32[]{:S(2)}) async-start(), calls=%async_computation.2 | async-start | bytes 1179648 | tf_op jit(solution)/shard_map/psum | solution.py:14
  267.3 29.5 %copy-start.1 = (f32[96,6,128]{2,0,1:T(8,128)S(1)}, f32[96,6,128]{2,0,1:T(8,128)}, u32[]{:S(2)}) copy-start(f32[96,6,128]{2,0,1:T(8,128)} %param.4) | copy-start | bytes 884740
  267.3 60.8 %all-to-all-start = ((f32[4,6,96,256]{3,0,1,2:T(4,128)}), f32[4,6,96,256]{3,0,1,2:T(4,128)S(1)}, u32[]{:S(2)}, u32[]{:S(2)}) async-start(f32[4,6,96,256]{3,0,1,2:T(4,128)} %copy.24), calls=%async_computation | async-start | bytes 4718592 | tf_op jit(solution)/shard_map/all_to_all | solution.py:56
  385.6 1.1 copy-start
Sparse Core Ops, SparseCore 0:
  10.3 245.2 all-reduce.1
where the time goes:
time: 397 us; the launch traced here: 396 us
  waiting for transfers between devices  278 us (70%)
  blocking collectives  37.5 us (9%)
  starting transfers between devices  29.5 us (7%)
  matrix products  25.4 us (6%)
  between operations  14.2 us (4%)
  local copies, waits for them, and re-layouts  6.07 us (2%)
  other arithmetic  5.19 us (1%)
    psum x1, waiting for transfers between devices, broadcast(): return lax.psum(block, axis)  247 us
    all_to_all x1, blocking collectives, local(): lax.all_to_all(spectral_spectrum, 'grid', split_axis=1, concat_axis=2, ti...  37.5 us
    all_to_all x1, waiting for transfers between devices, local(): lax.all_to_all(spectrum, 'grid', split_axis=2, concat_axis=1, tiled=True)  31.2 us
    all_to_all x1, starting transfers between devices, local(): lax.all_to_all(spectrum, 'grid', split_axis=2, concat_axis=1, tiled=True)  29.5 us
    dot_general x4, matrix products, along_dim(): jnp.einsum(letters, sine_part, spectrum, precision=precise, preferred_ele...  10.7 us
    dot_general x4, matrix products, along_dim(): jnp.einsum(letters, cosine, spectrum, precision=precise, preferred_elemen...  10.7 us
  transfers between devices with their start and end apart: 2, of which 2 were waited for; matrix products, arithmetic and copies ran while one was open for 0% of the time, Pallas kernels for 0%

commit v1 on v0

v1 whole, which is shorter than its diff:
```python
import math

import jax
import jax.numpy as jnp
from jax import lax
from jax.sharding import Mesh, PartitionSpec as P

precise = lax.Precision.HIGH
mixing = 0.25
band_axes = ("z", "y_lo")
grid_axes = ("x", "y_hi", "core")


def broadcast(block, holder):
    planes, pair = lax.axis_size("z"), lax.axis_size("y_lo")
    holder_z, holder_y = holder // pair, holder % pair
    mine = lax.axis_index("y_lo")
    rows = block.reshape(pair, planes, -1, block.shape[-1])
    swap = [(0, 1), (1, 0)]
    kept = lax.dynamic_index_in_dim(rows, mine, 0, keepdims=False)
    other = lax.dynamic_index_in_dim(rows, 1 - mine, 0, keepdims=False)
    received = lax.ppermute(other, "y_lo", swap)
    half = jnp.where(mine == holder_y, kept, received)
    pieces = lax.all_to_all(half, "z", 0, 0, tiled=True)
    piece = lax.dynamic_index_in_dim(pieces, holder_z, 0, keepdims=True)
    half = lax.all_to_all(jnp.broadcast_to(piece, half.shape), "z", 0, 0, tiled=True)
    partner = lax.ppermute(half, "y_lo", swap)
    low = jnp.where(mine == 0, half, partner)
    high = jnp.where(mine == 0, partner, half)
    return jnp.stack([low, high]).reshape(block.shape)


def twiddle(length):
    counter = jnp.arange(length, dtype=jnp.int32)
    phases = counter[:, None] * counter[None, :] % length
    angles = phases.astype(jnp.float32) * (2.0 * math.pi / length)
    return (jnp.cos(angles), jnp.sin(angles))


def along_dim(spectrum, cosine, sine_part, letters, forward):
    with_cosine = jnp.einsum(
        letters, cosine, spectrum, precision=precise, preferred_element_type=jnp.float32
    )
    with_sine = jnp.einsum(
        letters, sine_part, spectrum, precision=precise, preferred_element_type=jnp.float32
    )
    middle = spectrum.shape[-1] // 2
    real_cosine, imag_cosine = (with_cosine[..., :middle], with_cosine[..., middle:])
    real_sine, imag_sine = (with_sine[..., :middle], with_sine[..., middle:])
    if forward:
        return jnp.concatenate([real_cosine + imag_sine, imag_cosine - real_sine], axis=-1)
    return jnp.concatenate([real_cosine - imag_sine, imag_cosine + real_sine], axis=-1)


def local(orbitals, kernel, owners):
    orb_count, slab_x, rows_y, cells_z = orbitals.shape
    full_x = slab_x * lax.axis_size(grid_axes)
    cosine_x, sine_x = twiddle(full_x)
    cosine_y, sine_y = twiddle(rows_y)
    cosine_z, sine_z = twiddle(cells_z)
    norm_scale = 1.0 / (full_x * rows_y * cells_z)
    kernel_pair = jnp.concatenate([kernel, kernel], axis=-1)
    wave_z = jnp.concatenate(
        [
            jnp.concatenate([cosine_z, -sine_z], axis=1),
            jnp.concatenate([sine_z, cosine_z], axis=1),
        ],
        axis=0,
    )
    source_block = broadcast(orbitals, owners[0])
    density = jnp.concatenate(
        [orbitals * source_block[0][None], orbitals * source_block[1][None]], axis=-1
    )
    spectrum = jnp.dot(density, wave_z, precision=precise, preferred_element_type=jnp.float32)
    spectrum = along_dim(spectrum, cosine_y, sine_y, "ky,bxyc->bxkc", True)
    columns = lax.all_to_all(spectrum, grid_axes, split_axis=2, concat_axis=1, tiled=True)
    spectral_spectrum = along_dim(columns, cosine_x, sine_x, "kx,bxyc->bkyc", True)
    spectral_spectrum = spectral_spectrum * kernel_pair
    spectral_spectrum = along_dim(spectral_spectrum, cosine_x, sine_x, "kx,bxyc->bkyc", False)
    spectrum = lax.all_to_all(spectral_spectrum, grid_axes, split_axis=1, concat_axis=2, tiled=True)
    spectrum = along_dim(spectrum, cosine_y, sine_y, "ky,bxyc->bxkc", False)
    potential = jnp.dot(
        spectrum, wave_z.T * norm_scale, precision=precise, preferred_element_type=jnp.float32
    )
    accumulated = (
        source_block[0][None] * potential[..., :cells_z]
        + source_block[1][None] * potential[..., cells_z:]
    )
    return -mixing * accumulated


def solution(mesh):
    pair = 2
    band, grid = mesh.shape["band"], mesh.shape["grid"]
    shape = (band // pair, pair, grid // (2 * pair), pair, 2)
    fine = Mesh(mesh.devices.reshape(shape), band_axes + grid_axes)
    return jax.shard_map(
        local,
        mesh=fine,
        in_specs=(P(band_axes, grid_axes, None, None), P(None, grid_axes, None), P()),
        out_specs=P(band_axes, grid_axes, None, None),
        check_vma=False,
    )
```

time: 397 us -> 148 us (0.37)
  waiting for transfers between devices: 278 us -> 40 us
  matrix products: 25.4 us -> 8.04 us
  between operations: 14.2 us -> 0.96 us
  blocking collectives: 37.5 us -> 49.3 us
  starting transfers between devices: 29.5 us -> 40.6 us
    psum x1 -> x0, waiting for transfers between devices: 247 us -> none  [broadcast(): return lax.psum(block, axis)]
    all_to_all x1 -> x2, blocking collectives: 37.5 us -> 49.3 us  [the longest x1 26.3 us: broadcast(): lax.all_to_all(jnp.broadcast_to(piece, half.shape), 'z', 0, 0, tiled=True)]
    ppermute x0 -> x2, waiting for transfers between devices: none -> 7.47 us  [the longest x1 4.04 us: broadcast(): partner = lax.ppermute(half, 'y_lo', swap)]
    dot_general x4, matrix products: 10.7 us -> 3.36 us  [along_dim(): jnp.einsum(letters, sine_part, spectrum, precision=precise, preferred_ele...]
    dot_general x4, matrix products: 10.7 us -> 3.36 us  [along_dim(): jnp.einsum(letters, cosine, spectrum, precision=precise, preferred_elemen...]
    ppermute x0 -> x2, starting transfers between devices: none -> 7.23 us  [the longest x1 4.03 us: broadcast(): received = lax.ppermute(other, 'y_lo', swap)]
    all_to_all x1 -> x2, starting transfers between devices: 29.5 us -> 33.4 us  [the longest x1 17.4 us: broadcast(): pieces = lax.all_to_all(half, 'z', 0, 0, tiled=True)]
    all_to_all x1 -> x2, waiting for transfers between devices: 31.2 us -> 32.5 us  [the longest x1 18.6 us: local(): lax.all_to_all(spectrum, grid_axes, split_axis=2, concat_axis=1, tiled=True)]
  transfers between devices with their start and end apart: 2 -> 4, of which waited for: 2 -> 4; matrix products, arithmetic and copies ran while one was open for 0% -> 0% of each run, Pallas kernels for 0% -> 0%
where the time goes in v1:
time: 148 us
  blocking collectives  49.3 us (33%)
  starting transfers between devices  40.6 us (27%)
  waiting for transfers between devices  40 us (27%)
  matrix products  8.04 us (5%)
  local copies, waits for them, and re-layouts  6.62 us (4%)
  other arithmetic  2.37 us (2%)
    all_to_all x1, blocking collectives, broadcast(): lax.all_to_all(jnp.broadcast_to(piece, half.shape), 'z', 0, 0, tiled=True)  26.3 us
    all_to_all x1, blocking collectives, local(): lax.all_to_all(spectral_spectrum, grid_axes, split_axis=1, concat_axis=2,...  23 us
    all_to_all x1, waiting for transfers between devices, local(): lax.all_to_all(spectrum, grid_axes, split_axis=2, concat_axis=1, tiled=True)  18.6 us
    all_to_all x1, starting transfers between devices, broadcast(): pieces = lax.all_to_all(half, 'z', 0, 0, tiled=True)  17.4 us
    all_to_all x1, starting transfers between devices, local(): lax.all_to_all(spectrum, grid_axes, split_axis=2, concat_axis=1, tiled=True)  16 us
    all_to_all x1, waiting for transfers between devices, broadcast(): pieces = lax.all_to_all(half, 'z', 0, 0, tiled=True)  14 us
    ppermute x1, waiting for transfers between devices, broadcast(): partner = lax.ppermute(half, 'y_lo', swap)  4.04 us
    ppermute x1, starting transfers between devices, broadcast(): received = lax.ppermute(other, 'y_lo', swap)  4.03 us
  transfers between devices with their start and end apart: 4, of which 4 were waited for; matrix products, arithmetic and copies ran while one was open for 0% of the time, Pallas kernels for 0%

profile of v1, /device:TPU:1, one launch (start us, length us, event | category | flops | bytes accessed | tf_op | source)
XLA Modules:
  0.0 147.9 jit_solution(3712630208048854940)
XLA Ops:
  0.0 1.5 %copy.40 = f32[2,6,96,128]{3,0,2,1:T(2,128)S(1)} copy(f32[2,6,96,128]{3,2,1,0:T(8,128)} %param.3) | data formatting | bytes 1179648 | tf_op args[0]
  1.5 0.5 constant_dynamic-slice_fusion.1
  2.1 4.0 %collective-permute-start = (f32[16,36,128]{2,0,1:T(8,128)S(1)}, f32[16,36,128]{2,0,1:T(8,128)S(1)}, u32[]{:S(2)}, u32[]{:S(2)}) collective-permute-start(f32[16,36,128]{2,0,1:T(8,128)S(1)} %bitcast.78), channel_id=1, source_target_pairs={{0,16},{16,0},{1,17},{17,1},{2,18},{18,2},{3,19},{19,3},{4,20},{20... | collective-permute-start | bytes 884744 | tf_op jit(solution)/shard_map/ppermute | solution.py:22
  6.8 3.4 %collective-permute-done = f32[16,36,128]{2,0,1:T(8,128)S(1)} collective-permute-done((f32[16,36,128]{2,0,1:T(8,128)S(1)}, f32[16,36,128]{2,0,1:T(8,128)S(1)}, u32[]{:S(2)}, u32[]{:S(2)}) %collective-permute-start) | collective-permute-done | bytes 294944 | tf_op jit(solution)/shard_map/ppermute | solution.py:22
  10.3 0.8 copy.43
  11.1 17.4 %all-to-all-start = ((f32[16,36,128]{2,1,0:T(8,128)}), f32[16,36,128]{2,1,0:T(8,128)S(1)}, u32[]{:S(2)}, u32[]{:S(2)}) async-start(f32[16,36,128]{2,1,0:T(8,128)} %copy.43), calls=%async_computation | async-start | bytes 655360 | tf_op jit(solution)/shard_map/all_to_all | solution.py:24
  28.5 14.0 %all-to-all-done = f32[16,36,128]{2,1,0:T(8,128)S(1)} async-done(((f32[16,36,128]{2,1,0:T(8,128)}), f32[16,36,128]{2,1,0:T(8,128)S(1)}, u32[]{:S(2)}, u32[]{:S(2)}) %all-to-all-start) | async-done | bytes 294944 | tf_op jit(solution)/shard_map/all_to_all | solution.py:24
  42.5 26.3 %all_to_all.46 = f32[16,36,128]{2,1,0:T(8,128)S(1)} all-to-all(f32[16,36,128]{2,1,0:T(8,128)S(1)} %broadcast_in_dim.5), channel_id=1, replica_groups=mesh['z'=16,'y_lo'=2,'x'=4,'y_hi'=2,'core'=2] {'z'}, dimensions={0} | all-to-all | bytes 589824 | tf_op jit(solution)/shard_map/all_to_all | solution.py:26
  68.8 3.2 %collective-permute-start.1 = (f32[16,36,128]{2,1,0:T(8,128)S(1)}, f32[16,36,128]{2,1,0:T(8,128)S(1)}, u32[]{:S(2)}, u32[]{:S(2)}) collective-permute-start(f32[16,36,128]{2,1,0:T(8,128)S(1)} %all_to_all.46), channel_id=1, source_target_pairs={{0,16},{16,0},{1,17},{17,1},{2,18},{18,2},{3,19},{19,3},{4,20},{20... | collective-permute-start | bytes 884744 | tf_op jit(solution)/shard_map/ppermute | solution.py:27
  72.0 0.3 fusion.49
  72.3 0.3 fusion.50
  72.6 4.0 %collective-permute-done.1 = f32[16,36,128]{2,1,0:T(8,128)S(1)} collective-permute-done((f32[16,36,128]{2,1,0:T(8,128)S(1)}, f32[16,36,128]{2,1,0:T(8,128)S(1)}, u32[]{:S(2)}, u32[]{:S(2)}) %collective-permute-start.1) | collective-permute-done | bytes 294944 | tf_op jit(solution)/shard_map/ppermute | solution.py:27
  76.9 0.6 fusion
  77.5 0.8 convolution_bitcast_fusion.6
  78.3 0.8 convolution_bitcast_fusion.7
  79.2 0.1 slice_add_fusion.3
  79.4 1.9 %copy.44 = f32[2,6,96,256]{3,0,1,2:T(2,128)} copy(f32[2,6,96,256]{3,2,1,0:T(8,128)S(1)} %pad_maximum_fusion) | data formatting | bytes 2359296 | tf_op jit(solution)/shard_map/concatenate | solution.py:51
  81.3 16.0 %all-to-all-start.2 = ((f32[2,6,96,256]{3,0,1,2:T(2,128)}), f32[2,6,96,256]{3,0,1,2:T(2,128)S(1)}, u32[]{:S(2)}, u32[]{:S(2)}) async-start(f32[2,6,96,256]{3,0,1,2:T(2,128)} %copy.44), calls=%async_computation.2 | async-start | bytes 2359296 | tf_op jit(solution)/shard_map/all_to_all | solution.py:76
  97.4 18.6 %all-to-all-done.2 = f32[2,6,96,256]{3,0,1,2:T(2,128)S(1)} async-done(((f32[2,6,96,256]{3,0,1,2:T(2,128)}), f32[2,6,96,256]{3,0,1,2:T(2,128)S(1)}, u32[]{:S(2)}, u32[]{:S(2)}) %all-to-all-start.2) | async-done | bytes 1179680 | tf_op jit(solution)/shard_map/all_to_all | solution.py:76
  116.0 0.4 copy.46
  116.4 0.9 convolution_bitcast_fusion.4
  117.3 0.9 convolution_bitcast_fusion.5
  118.3 0.9 convolution_bitcast_fusion.3
  119.2 0.8 convolution_bitcast_fusion.2
  120.0 0.1 slice_subtract_fusion.1
  120.3 0.9 copy.49
  121.2 23.0 %all_to_all.47 = f32[2,96,6,256]{3,0,2,1:T(2,128)S(1)} all-to-all(f32[2,96,6,256]{3,0,2,1:T(2,128)S(1)} %copy.49), channel_id=1, replica_groups=mesh['z'=16,'y_lo'=2,'x'=4,'y_hi'=2,'core'=2] {'x','y_hi','core'}, dimensions={1} | all-to-all | bytes 2359296 | tf_op jit(solution)/shard_map/all_to_all | solution.py:80
  144.1 0.4 copy.50
  144.6 0.8 convolution_bitcast_fusion
  145.4 0.8 convolution_bitcast_fusion.1
  146.3 0.7 fusion.4
  147.0 0.9 fusion.13
  (17 shorter events, 0.7 us)
Async XLA Ops:
  2.1 8.1 %collective-permute-start = (f32[16,36,128]{2,0,1:T(8,128)S(1)}, f32[16,36,128]{2,0,1:T(8,128)S(1)}, u32[]{:S(2)}, u32[]{:S(2)}) collective-permute-start(f32[16,36,128]{2,0,1:T(8,128)S(1)} %bitcast.78), channel_id=1, source_target_pairs={{0,16},{16,0},{1,17},{17,1},{2,18},{18,2},{3,19},{19,3},{4,20},{20... | collective-permute-start | bytes 884744 | tf_op jit(solution)/shard_map/ppermute | solution.py:22
  11.1 31.4 %all-to-all-start = ((f32[16,36,128]{2,1,0:T(8,128)}), f32[16,36,128]{2,1,0:T(8,128)S(1)}, u32[]{:S(2)}, u32[]{:S(2)}) async-start(f32[16,36,128]{2,1,0:T(8,128)} %copy.43), calls=%async_computation | async-start | bytes 655360 | tf_op jit(solution)/shard_map/all_to_all | solution.py:24
  68.8 7.8 %collective-permute-start.1 = (f32[16,36,128]{2,1,0:T(8,128)S(1)}, f32[16,36,128]{2,1,0:T(8,128)S(1)}, u32[]{:S(2)}, u32[]{:S(2)}) collective-permute-start(f32[16,36,128]{2,1,0:T(8,128)S(1)} %all_to_all.46), channel_id=1, source_target_pairs={{0,16},{16,0},{1,17},{17,1},{2,18},{18,2},{3,19},{19,3},{4,20},{20... | collective-permute-start | bytes 884744 | tf_op jit(solution)/shard_map/ppermute | solution.py:27
  72.6 4.2 %copy-start = (f32[2,6,96,128]{3,2,1,0:T(8,128)S(1)}, f32[2,6,96,128]{3,2,1,0:T(8,128)}, u32[]{:S(2)}) copy-start(f32[2,6,96,128]{3,2,1,0:T(8,128)} %param.3) | copy-start | bytes 1769476
  81.3 16.0 %copy-start.1 = (f32[96,6,128]{2,0,1:T(8,128)S(1)}, f32[96,6,128]{2,0,1:T(8,128)}, u32[]{:S(2)}) copy-start(f32[96,6,128]{2,0,1:T(8,128)} %param.4) | copy-start | bytes 884740
  81.3 34.7 %all-to-all-start.2 = ((f32[2,6,96,256]{3,0,1,2:T(2,128)}), f32[2,6,96,256]{3,0,1,2:T(2,128)S(1)}, u32[]{:S(2)}, u32[]{:S(2)}) async-start(f32[2,6,96,256]{3,0,1,2:T(2,128)} %copy.44), calls=%async_computation.2 | async-start | bytes 2359296 | tf_op jit(solution)/shard_map/all_to_all | solution.py:76

commit v2 on v0

v2 whole, which is shorter than its diff:
```python
import functools

import jax
import jax.numpy as jnp
import numpy as np
from jax import lax
from jax.experimental import pallas as pl
from jax.experimental.pallas import tpu as pltpu
from jax.sharding import Mesh, PartitionSpec as P

mixing = 0.25
pair = 2
far_axis = "z_far"
near_axes = ("z_near", "y_lo")
band_axes = (far_axis,) + near_axes
grid_axes = ("x", "y_hi", "core")
lanes = 128


def pieces_of(block, axes, holder):
    pieces = block.reshape(lax.axis_size(axes), -1, block.shape[-1])
    received = lax.all_to_all(pieces, axes, 0, 0, tiled=True)
    return lax.dynamic_index_in_dim(received, holder, 0, keepdims=False)


def copies_of(piece, axes):
    copies = jnp.broadcast_to(piece[None], (lax.axis_size(axes),) + piece.shape)
    return lax.all_to_all(copies, axes, 0, 0, tiled=True)


def broadcast(block, holder):
    members = lax.axis_size(near_axes)
    piece = pieces_of(block, near_axes, holder % members)
    everywhere = copies_of(piece, far_axis)
    piece = lax.dynamic_index_in_dim(everywhere, holder // members, 0, keepdims=False)
    return copies_of(piece, near_axes).reshape(block.shape)


def wave(length, forward):
    counter = np.arange(length)
    angles = 2.0 * np.pi * (np.outer(counter, counter) % length) / length
    cosine, sine = np.cos(angles), np.sin(angles)
    if not forward:
        sine = -sine
    return np.block([[cosine, sine], [-sine, cosine]])


def spread(length, parts):
    order = np.arange(length).reshape(parts, -1).T.reshape(-1)
    return np.concatenate([order, order + length])


def halves(matrix):
    upper = matrix.astype(jnp.bfloat16)
    return upper, (matrix - upper.astype(np.float64)).astype(jnp.bfloat16)


def split(values):
    upper = values.astype(jnp.bfloat16)
    return upper, (values - upper.astype(jnp.float32)).astype(jnp.bfloat16)


def times(left, right):
    dot = functools.partial(jnp.dot, preferred_element_type=jnp.float32)
    return dot(left[0], right[0]) + dot(left[0], right[1]) + dot(left[1], right[0])


def both(pair_refs):
    return pair_refs[0][...], pair_refs[1][...]


def at(column):
    return slice(column * lanes, (column + 1) * lanes)


def to_columns(parts, orbitals, block, z_up, z_low, y_up, y_low, sent):
    orb_count, slab, rows, _ = orbitals.shape
    share = rows // parts
    stride = sent.shape[0] // parts
    wave_z, wave_y = both((z_up, z_low)), both((y_up, y_low))
    for orb in range(orb_count):
        density = jnp.concatenate([orbitals[orb] * block[0], orbitals[orb] * block[1]], axis=-1)
        spectrum = times(split(density.reshape(slab * rows, 2 * lanes)), wave_z)
        spectrum = spectrum.reshape(slab, rows, 2 * lanes)
        stacked = jnp.concatenate(
            [
                jnp.concatenate([spectrum[plane, :, :lanes], spectrum[plane, :, lanes:]], axis=0)
                for plane in range(slab)
            ],
            axis=1,
        )
        columns = times(wave_y, split(stacked))
        for part in range(2):
            for plane in range(slab):
                first = ((orb * 2 + part) * slab + plane) * share
                for place in range(share):
                    start = (part * share + place) * parts
                    sent[pl.ds(first + place, parts, stride), :] = columns[
                        start : start + parts, at(plane)
                    ]


def in_columns(parts, received, weights, f_up, f_low, i_up, i_low, sent):
    stride = received.shape[0] // parts
    group = f_up.shape[0] // parts
    share = weights.shape[1] // lanes
    forward, inverse = both((f_up, f_low)), both((i_up, i_low))
    scale = jnp.concatenate([weights[...]] * 2, axis=0)
    for orb in range(stride // (group * share)):
        first = orb * group * share
        stacked = jnp.concatenate(
            [
                jnp.concatenate(
                    [
                        received[pl.ds(first + row * share + place, parts, stride), :]
                        for place in range(share)
                    ],
                    axis=1,
                )
                for row in range(group)
            ],
            axis=0,
        )
        spectral = times(forward, split(stacked)) * scale
        planes = times(inverse, split(spectral))
        for row in range(group):
            for place in range(share):
                sent[pl.ds(first + row * share + place, parts, stride), :] = planes[
                    row * parts : (row + 1) * parts, at(place)
                ]


def from_columns(parts, received, block, y_up, y_low, z_up, z_low, out):
    orb_count, slab, rows, _ = out.shape
    share = rows // parts
    stride = received.shape[0] // parts
    wave_y, wave_z = both((y_up, y_low)), both((z_up, z_low))
    for orb in range(orb_count):
        stacked = jnp.concatenate(
            [
                jnp.concatenate(
                    [
                        received[
                            pl.ds(
                                ((orb * 2 + part) * slab + plane) * share + place, parts, stride
                            ),
                            :,
                        ]
                        for part in range(2)
                        for place in range(share)
                    ],
                    axis=0,
                )
                for plane in range(slab)
            ],
            axis=1,
        )
        spectrum = times(wave_y, split(stacked))
        spectrum = jnp.concatenate(
            [
                jnp.concatenate([spectrum[:rows, at(plane)], spectrum[rows:, at(plane)]], axis=1)
                for plane in range(slab)
            ],
            axis=0,
        )
        potential = times(split(spectrum), wave_z).reshape(slab, rows, 2 * lanes)
        out[orb] = block[0] * potential[..., :lanes] + block[1] * potential[..., lanes:]


def on_device(body, shape, flops, *operands):
    moved = sum(x.size * x.dtype.itemsize for x in operands) + 4 * int(np.prod(shape))
    return pl.pallas_call(
        body,
        out_shape=jax.ShapeDtypeStruct(shape, jnp.float32),
        in_specs=[pl.BlockSpec(memory_space=pltpu.VMEM)] * len(operands),
        out_specs=pl.BlockSpec(memory_space=pltpu.VMEM),
        compiler_params=pltpu.CompilerParams(vmem_limit_bytes=32 * 1024 * 1024),
        cost_estimate=pl.CostEstimate(flops=flops, bytes_accessed=moved, transcendentals=0),
    )(*operands)


def local(orbitals, kernel, owners):
    orb_count, slab, rows, cells = orbitals.shape
    parts = lax.axis_size(grid_axes)
    full = slab * parts
    share = rows // parts
    order_x, order_y = spread(full, parts), spread(rows, parts)
    forward_z = halves(wave(cells, True).T)
    inverse_z = halves(wave(cells, False).T * (-mixing / (full * rows * cells)))
    forward_y = halves(wave(rows, True)[order_y])
    inverse_y = halves(wave(rows, False)[:, order_y])
    forward_x = halves(wave(full, True)[order_x][:, order_x])
    inverse_x = halves(wave(full, False)[order_x][:, order_x])
    weights = kernel.reshape(parts, slab, share * cells).swapaxes(0, 1).reshape(full, share * cells)

    source_block = broadcast(orbitals, owners[0])
    sent_rows = orb_count * 2 * slab * share
    shape = (parts * sent_rows, cells)
    points = orb_count * slab * rows * cells

    def exchange(columns):
        columns = columns.reshape(parts, sent_rows, cells)
        return lax.all_to_all(columns, grid_axes, 0, 0, tiled=True).reshape(shape)

    columns = on_device(
        functools.partial(to_columns, parts),
        shape,
        24 * points * (cells + rows),
        orbitals,
        source_block,
        *forward_z,
        *forward_y,
    )
    columns = exchange(columns)
    columns = on_device(
        functools.partial(in_columns, parts),
        shape,
        48 * points * full,
        columns,
        weights,
        *forward_x,
        *inverse_x,
    )
    columns = exchange(columns)
    return on_device(
        functools.partial(from_columns, parts),
        orbitals.shape,
        24 * points * (cells + rows),
        columns,
        source_block,
        *inverse_y,
        *inverse_z,
    )


def solution(mesh):
    band, grid = mesh.shape["band"], mesh.shape["grid"]
    shape = (band // (4 * pair), 4, pair, grid // (2 * pair), pair, 2)
    fine = Mesh(mesh.devices.reshape(shape), band_axes + grid_axes)
    return jax.shard_map(
        local,
        mesh=fine,
        in_specs=(P(band_axes, grid_axes, None, None), P(None, grid_axes, None), P()),
        out_specs=P(band_axes, grid_axes, None, None),
        check_vma=False,
    )
```

time: 397 us -> 131 us (0.33)
  waiting for transfers between devices: 278 us -> 45.5 us
  matrix products: 25.4 us -> 0 us
  between operations: 14.2 us -> 0.84 us
  Pallas kernels: 0 us -> 7.57 us
  other arithmetic: 5.19 us -> 0 us
  local copies, waits for them, and re-layouts: 6.07 us -> 1.21 us
  blocking collectives: 37.5 us -> 42 us
    psum x1 -> x0, waiting for transfers between devices: 247 us -> none  [broadcast(): return lax.psum(block, axis)]
    dot_general x10 -> x0, matrix products: 25.4 us -> none  [the longest x4 10.7 us: along_dim(): jnp.einsum(letters, sine_part, spectrum, precision=precise, preferred_ele...]
    all_to_all x1 -> x3, waiting for transfers between devices: 31.2 us -> 45.5 us  [the longest x1 18.2 us: exchange(): return lax.all_to_all(columns, grid_axes, 0, 0, tiled=True).reshape(shape)]
    pallas_call x0 -> x3, Pallas kernels: none -> 7.57 us  [on_device(): pl.pallas_call(body, out_shape=jax.ShapeDtypeStruct(shape, jnp.float32),...]
    all_to_all x1 -> x2, blocking collectives: 37.5 us -> 42 us  [the longest x1 23.1 us: exchange(): return lax.all_to_all(columns, grid_axes, 0, 0, tiled=True).reshape(shape)]
    concatenate x2 -> x0, local copies, waits for them, and re-layouts: 4.45 us -> none  [the longest x1 2.93 us: along_dim(): jnp.concatenate([real_cosine + imag_sine, imag_cosine - real_sine], axis=-1)]
    all_to_all x1 -> x3, starting transfers between devices: 29.5 us -> 33.4 us  [the longest x1 15.4 us: copies_of(): return lax.all_to_all(copies, axes, 0, 0, tiled=True)]
  transfers between devices with their start and end apart: 2 -> 3, of which waited for: 2 -> 3; matrix products, arithmetic and copies ran while one was open for 0% -> 0% of each run, Pallas kernels for 0% -> 0%
where the time goes in v2:
time: 131 us; the launch traced here: 130 us
  waiting for transfers between devices  45.5 us (35%)
  blocking collectives  42 us (32%)
  starting transfers between devices  33.4 us (25%)
  Pallas kernels  7.57 us (6%)
    all_to_all x1, blocking collectives, exchange(): return lax.all_to_all(columns, grid_axes, 0, 0, tiled=True).reshape(shape)  23.1 us
    all_to_all x1, blocking collectives, copies_of(): return lax.all_to_all(copies, axes, 0, 0, tiled=True)  18.9 us
    all_to_all x1, waiting for transfers between devices, exchange(): return lax.all_to_all(columns, grid_axes, 0, 0, tiled=True).reshape(shape)  18.2 us
    all_to_all x1, waiting for transfers between devices, copies_of(): return lax.all_to_all(copies, axes, 0, 0, tiled=True)  16.4 us
    all_to_all x1, starting transfers between devices, copies_of(): return lax.all_to_all(copies, axes, 0, 0, tiled=True)  15.4 us
    all_to_all x1, waiting for transfers between devices, pieces_of(): received = lax.all_to_all(pieces, axes, 0, 0, tiled=True)  10.9 us
    all_to_all x1, starting transfers between devices, exchange(): return lax.all_to_all(columns, grid_axes, 0, 0, tiled=True).reshape(shape)  10.5 us
    pallas_call x3, Pallas kernels, on_device(): pl.pallas_call(body, out_shape=jax.ShapeDtypeStruct(shape, jnp.float32),...  7.57 us
  transfers between devices with their start and end apart: 3, of which 3 were waited for; matrix products, arithmetic and copies ran while one was open for 0% of the time, Pallas kernels for 0%

profile of v2, /device:TPU:1, one launch (start us, length us, event | category | flops | bytes accessed | tf_op | source)
XLA Modules:
  0.0 130.5 jit_solution(4589275578713855488)
XLA Ops:
  0.0 7.5 %all-to-all-start = ((f32[8,144,128]{2,1,0:T(8,128)}), f32[8,144,128]{2,1,0:T(8,128)S(1)}, u32[]{:S(2)}, u32[]{:S(2)}) async-start(f32[8,144,128]{2,1,0:T(8,128)} %bitcast.21), calls=%async_computation | async-start | bytes 1179648 | tf_op jit(solution)/shard_map/all_to_all | solution.py:22
  8.1 10.9 %all-to-all-done = f32[8,144,128]{2,1,0:T(8,128)S(1)} async-done(((f32[8,144,128]{2,1,0:T(8,128)}), f32[8,144,128]{2,1,0:T(8,128)S(1)}, u32[]{:S(2)}, u32[]{:S(2)}) %all-to-all-start) | async-done | bytes 589856 | tf_op jit(solution)/shard_map/all_to_all | solution.py:22
  19.0 0.7 broadcast_in_dim.17
  19.8 0.0 copy-start.12
  19.8 15.4 %all-to-all-start.1 = ((f32[4,144,128]{2,1,0:T(8,128)}), f32[4,144,128]{2,1,0:T(8,128)S(1)}, u32[]{:S(2)}, u32[]{:S(2)}) async-start(f32[4,144,128]{2,1,0:T(8,128)} %broadcast_in_dim.17), calls=%async_computation.1 | async-start | bytes 589824 | tf_op jit(solution)/shard_map/all_to_all | solution.py:28
  35.2 16.4 %all-to-all-done.1 = f32[4,144,128]{2,1,0:T(8,128)S(1)} async-done(((f32[4,144,128]{2,1,0:T(8,128)}), f32[4,144,128]{2,1,0:T(8,128)S(1)}, u32[]{:S(2)}, u32[]{:S(2)}) %all-to-all-start.1) | async-done | bytes 294944 | tf_op jit(solution)/shard_map/all_to_all | solution.py:28
  51.6 18.9 %all_to_all.25 = f32[8,144,128]{2,1,0:T(8,128)S(1)} all-to-all(f32[8,144,128]{2,1,0:T(8,128)S(1)} %broadcast_in_dim.19), channel_id=1, replica_groups=mesh['z_far'=4,'z_near'=4,'y_lo'=2,'x'=4,'y_hi'=2,'core'=2] {'z_near','y..., dimensions={0} | all-to-all | bytes 1179648 | tf_op jit(solution)/shard_map/all_to_all | solution.py:28
  70.5 0.0 copy-done
  70.5 0.0 copy-done.7
  70.5 0.0 copy-done.8
  70.5 0.0 copy-done.11
  70.6 0.0 copy-done.12
  70.6 3.3 %shard_map.145 = f32[2304,128]{1,0:T(8,128)} custom-call(f32[2,6,96,128]{3,2,1,0:T(8,128)S(1)} %copy-done, f32[2,6,96,128]{3,2,1,0:T(8,128)S(1)} %bitcast.22, bf16[256,256]{1,0:T(8,128)(2,1)S(1)} %copy-done.7, bf16[256,256]{1,0:T(8,128)(2,1)S(1)} %copy-done.8, bf16[192,192]{1,0:T(8,128)(2,1)S(1)} %copy-done.11, bf16[192,192]{1,0:T(8,128)(2,1)S(1)} %copy-done.12), custom_call_target="tpu_custom_call" | custom-call | flops 792723456 | bytes 2768896 | tf_op jit(solution)/shard_map/pallas_call | solution.py:172
  73.8 10.5 %all-to-all-start.3 = ((f32[16,144,128]{2,1,0:T(8,128)}), f32[16,144,128]{2,1,0:T(8,128)S(1)}, u32[]{:S(2)}, u32[]{:S(2)}) async-start(f32[16,144,128]{2,1,0:T(8,128)} %bitcast.5), calls=%async_computation.3 | async-start | bytes 2359296 | tf_op jit(solution)/shard_map/all_to_all | solution.py:203
  84.4 0.0 copy-done.13
  84.4 0.0 copy-start.1
  84.4 0.0 copy-start.2
  84.4 0.0 copy-start.3
  84.4 0.0 copy-start.4
  84.4 0.2 copy.16
  84.6 0.1 reshape.28
  84.7 0.1 copy.17
  84.8 18.2 %all-to-all-done.3 = f32[16,144,128]{2,1,0:T(8,128)S(1)} async-done(((f32[16,144,128]{2,1,0:T(8,128)}), f32[16,144,128]{2,1,0:T(8,128)S(1)}, u32[]{:S(2)}, u32[]{:S(2)}) %all-to-all-start.3) | async-done | bytes 1179680 | tf_op jit(solution)/shard_map/all_to_all | solution.py:203
  103.0 0.0 copy-done.4
  103.0 1.8 %shard_map.146 = f32[2304,128]{1,0:T(8,128)S(1)} custom-call(f32[2304,128]{1,0:T(8,128)S(1)} %bitcast.17, f32[96,768]{1,0:T(8,128)S(1)} %bitcast.19, bf16[192,192]{1,0:T(8,128)(2,1)S(1)} %copy-done.1, bf16[192,192]{1,0:T(8,128)(2,1)S(1)} %copy-done.2, bf16[192,192]{1,0:T(8,128)(2,1)S(1)} %copy-done.3, bf16[192,192]{1,0:T(8,128)(2,1)S(1)} %copy-done.4), custom_call_target="tpu_custom_call" | custom-call | flops 679477248 | bytes 2949120 | tf_op jit(solution)/shard_map/pallas_call | solution.py:172
  104.8 0.0 copy-start.5
  104.8 0.0 copy-start.6
  104.8 0.0 copy-start.9
  104.8 0.0 copy-start.10
  104.8 23.1 %all_to_all.26 = f32[16,144,128]{2,1,0:T(8,128)S(1)} all-to-all(f32[16,144,128]{2,1,0:T(8,128)S(1)} %bitcast.18), channel_id=1, replica_groups=mesh['z_far'=4,'z_near'=4,'y_lo'=2,'x'=4,'y_hi'=2,'core'=2] {'x','y_hi',..., dimensions={0} | all-to-all | bytes 2359296 | tf_op jit(solution)/shard_map/all_to_all | solution.py:203
  127.9 0.0 copy-done.10
  127.9 2.6 %shard_map.147 = f32[2,6,96,128]{3,2,1,0:T(8,128)} custom-call(f32[2304,128]{1,0:T(8,128)S(1)} %bitcast.20, f32[2,6,96,128]{3,2,1,0:T(8,128)S(1)} %bitcast.23, bf16[192,192]{1,0:T(8,128)(2,1)S(1)} %copy-done.9, bf16[192,192]{1,0:T(8,128)(2,1)S(1)} %copy-done.10, bf16[256,256]{1,0:T(8,128)(2,1)S(1)} %copy-done.5, bf16[256,256]{1,0:T(8,128)(2,1)S(1)} %copy-done.6), custom_call_target="tpu_custom_call" | custom-call | flops 792723456 | bytes 2768896 | tf_op jit(solution)/shard_map/pallas_call | solution.py:172
  (14 shorter events, 0.1 us)
Async XLA Ops:
  0.0 19.0 %all-to-all-start = ((f32[8,144,128]{2,1,0:T(8,128)}), f32[8,144,128]{2,1,0:T(8,128)S(1)}, u32[]{:S(2)}, u32[]{:S(2)}) async-start(f32[8,144,128]{2,1,0:T(8,128)} %bitcast.21), calls=%async_computation | async-start | bytes 1179648 | tf_op jit(solution)/shard_map/all_to_all | solution.py:22
  19.8 50.8 %copy-start = (f32[2,6,96,128]{3,2,1,0:T(8,128)S(1)}, f32[2,6,96,128]{3,2,1,0:T(8,128)}, u32[]{:S(2)}) copy-start(f32[2,6,96,128]{3,2,1,0:T(8,128)} %orbitals.1) | copy-start | bytes 1769476
  19.8 50.8 %copy-start.7 = (bf16[256,256]{1,0:T(8,128)(2,1)S(1)}, bf16[256,256]{1,0:T(8,128)(2,1)}, u32[]{:S(2)}) copy-start(bf16[256,256]{1,0:T(8,128)(2,1)} %constant.59.clone.z_up) | copy-start | bytes 393220
  19.8 50.8 %copy-start.8 = (bf16[256,256]{1,0:T(8,128)(2,1)S(1)}, bf16[256,256]{1,0:T(8,128)(2,1)}, u32[]{:S(2)}) copy-start(bf16[256,256]{1,0:T(8,128)(2,1)} %constant.60.clone.z_low) | copy-start | bytes 393220
  19.8 50.8 %copy-start.11 = (bf16[192,192]{1,0:T(8,128)(2,1)S(1)}, bf16[192,192]{1,0:T(8,128)(2,1)}, u32[]{:S(2)}) copy-start(bf16[192,192]{1,0:T(8,128)(2,1)} %constant.61.clone.y_up) | copy-start | bytes 221188
  19.8 50.8 %copy-start.12 = (bf16[192,192]{1,0:T(8,128)(2,1)S(1)}, bf16[192,192]{1,0:T(8,128)(2,1)}, u32[]{:S(2)}) copy-start(bf16[192,192]{1,0:T(8,128)(2,1)} %constant.62.clone.y_low) | copy-start | bytes 221188
  19.8 31.8 %all-to-all-start.1 = ((f32[4,144,128]{2,1,0:T(8,128)}), f32[4,144,128]{2,1,0:T(8,128)S(1)}, u32[]{:S(2)}, u32[]{:S(2)}) async-start(f32[4,144,128]{2,1,0:T(8,128)} %broadcast_in_dim.17), calls=%async_computation.1 | async-start | bytes 589824 | tf_op jit(solution)/shard_map/all_to_all | solution.py:28
  73.8 10.5 %copy-start.13 = (f32[96,6,128]{2,0,1:T(8,128)S(1)}, f32[96,6,128]{2,0,1:T(8,128)}, u32[]{:S(2)}) copy-start(f32[96,6,128]{2,0,1:T(8,128)} %param.16) | copy-start | bytes 884740
  73.8 29.2 %all-to-all-start.3 = ((f32[16,144,128]{2,1,0:T(8,128)}), f32[16,144,128]{2,1,0:T(8,128)S(1)}, u32[]{:S(2)}, u32[]{:S(2)}) async-start(f32[16,144,128]{2,1,0:T(8,128)} %bitcast.5), calls=%async_computation.3 | async-start | bytes 2359296 | tf_op jit(solution)/shard_map/all_to_all | solution.py:203
  84.4 18.6 %copy-start.1 = (bf16[192,192]{1,0:T(8,128)(2,1)S(1)}, bf16[192,192]{1,0:T(8,128)(2,1)}, u32[]{:S(2)}) copy-start(bf16[192,192]{1,0:T(8,128)(2,1)} %constant.63.clone.f_up) | copy-start | bytes 221188
  84.4 18.6 %copy-start.2 = (bf16[192,192]{1,0:T(8,128)(2,1)S(1)}, bf16[192,192]{1,0:T(8,128)(2,1)}, u32[]{:S(2)}) copy-start(bf16[192,192]{1,0:T(8,128)(2,1)} %constant.64.clone.f_low) | copy-start | bytes 221188
  84.4 18.6 %copy-start.3 = (bf16[192,192]{1,0:T(8,128)(2,1)S(1)}, bf16[192,192]{1,0:T(8,128)(2,1)}, u32[]{:S(2)}) copy-start(bf16[192,192]{1,0:T(8,128)(2,1)} %constant.65.clone.i_up) | copy-start | bytes 221188
  84.4 18.6 %copy-start.4 = (bf16[192,192]{1,0:T(8,128)(2,1)S(1)}, bf16[192,192]{1,0:T(8,128)(2,1)}, u32[]{:S(2)}) copy-start(bf16[192,192]{1,0:T(8,128)(2,1)} %constant.66.clone.i_low) | copy-start | bytes 221188
  104.8 23.2 %copy-start.5 = (bf16[256,256]{1,0:T(8,128)(2,1)S(1)}, bf16[256,256]{1,0:T(8,128)(2,1)}, u32[]{:S(2)}) copy-start(bf16[256,256]{1,0:T(8,128)(2,1)} %constant.69.clone.z_up) | copy-start | bytes 393220
  104.8 23.1 %copy-start.6 = (bf16[256,256]{1,0:T(8,128)(2,1)S(1)}, bf16[256,256]{1,0:T(8,128)(2,1)}, u32[]{:S(2)}) copy-start(bf16[256,256]{1,0:T(8,128)(2,1)} %constant.70.clone.z_low) | copy-start | bytes 393220
  104.8 23.1 %copy-start.9 = (bf16[192,192]{1,0:T(8,128)(2,1)S(1)}, bf16[192,192]{1,0:T(8,128)(2,1)}, u32[]{:S(2)}) copy-start(bf16[192,192]{1,0:T(8,128)(2,1)} %constant.67.clone.y_up) | copy-start | bytes 221188
  104.8 23.1 %copy-start.10 = (bf16[192,192]{1,0:T(8,128)(2,1)S(1)}, bf16[192,192]{1,0:T(8,128)(2,1)}, u32[]{:S(2)}) copy-start(bf16[192,192]{1,0:T(8,128)(2,1)} %constant.68.clone.y_low) | copy-start | bytes 221188

commit v3 on v2

--- a/solution.py
+++ b/solution.py
@@ -28,12 +28,13 @@
     return lax.all_to_all(copies, axes, 0, 0, tiled=True)
 
 
-def broadcast(block, holder):
+def broadcast(block, holder, aside):
     members = lax.axis_size(near_axes)
     piece = pieces_of(block, near_axes, holder % members)
-    everywhere = copies_of(piece, far_axis)
+    piece, aside = lax.optimization_barrier((piece, aside))
+    everywhere = lax.all_gather(piece, far_axis, axis=0)
     piece = lax.dynamic_index_in_dim(everywhere, holder // members, 0, keepdims=False)
-    return copies_of(piece, near_axes).reshape(block.shape)
+    return copies_of(piece, near_axes).reshape(block.shape), aside
 
 
 def wave(length, forward):
@@ -193,7 +194,7 @@
     inverse_x = halves(wave(full, False)[order_x][:, order_x])
     weights = kernel.reshape(parts, slab, share * cells).swapaxes(0, 1).reshape(full, share * cells)
 
-    source_block = broadcast(orbitals, owners[0])
+    source_block, weights = broadcast(orbitals, owners[0], weights)
     sent_rows = orb_count * 2 * slab * share
     shape = (parts * sent_rows, cells)
     points = orb_count * slab * rows * cells

time: 131 us -> 123 us (0.939)
  blocking collectives: 42 us -> 96.8 us
  waiting for transfers between devices: 45.5 us -> 10.5 us
  starting transfers between devices: 33.4 us -> 7.59 us
    all_to_all x2 -> x0, waiting for transfers between devices: 34.6 us -> none  [the longest x1 18.2 us: exchange(): return lax.all_to_all(columns, grid_axes, 0, 0, tiled=True).reshape(shape)]
    all_gather x0 -> x1, blocking collectives: none -> 26.9 us  [broadcast(): everywhere = lax.all_gather(piece, far_axis, axis=0)]
    all_to_all x1 -> x2, blocking collectives: 23.1 us -> 49.9 us  [exchange(): return lax.all_to_all(columns, grid_axes, 0, 0, tiled=True).reshape(shape)]
    all_to_all x2 -> x0, starting transfers between devices: 25.9 us -> none  [the longest x1 15.4 us: copies_of(): return lax.all_to_all(copies, axes, 0, 0, tiled=True)]
  transfers between devices with their start and end apart: 3 -> 1, of which waited for: 3 -> 1; matrix products, arithmetic and copies ran while one was open for 0% -> 0% of each run, Pallas kernels for 0% -> 0%
where the time goes in v3:
time: 123 us
  blocking collectives  96.8 us (79%)
  waiting for transfers between devices  10.5 us (9%)
  starting transfers between devices  7.59 us (6%)
  Pallas kernels  6.51 us (5%)
    all_to_all x2, blocking collectives, exchange(): return lax.all_to_all(columns, grid_axes, 0, 0, tiled=True).reshape(shape)  49.9 us
    all_gather x1, blocking collectives, broadcast(): everywhere = lax.all_gather(piece, far_axis, axis=0)  26.9 us
    all_to_all x1, blocking collectives, copies_of(): return lax.all_to_all(copies, axes, 0, 0, tiled=True)  20 us
    all_to_all x1, waiting for transfers between devices, pieces_of(): received = lax.all_to_all(pieces, axes, 0, 0, tiled=True)  10.5 us
    all_to_all x1, starting transfers between devices, pieces_of(): received = lax.all_to_all(pieces, axes, 0, 0, tiled=True)  7.59 us
    pallas_call x3, Pallas kernels, on_device(): pl.pallas_call(body, out_shape=jax.ShapeDtypeStruct(shape, jnp.float32),...  6.51 us
  transfers between devices with their start and end apart: 1, of which 1 were waited for; matrix products, arithmetic and copies ran while one was open for 0% of the time, Pallas kernels for 0%

profile of v3, /device:TPU:1, one launch (start us, length us, event | category | flops | bytes accessed | tf_op | source)
XLA Modules:
  0.0 122.8 jit_solution(3429358465117744209)
XLA Ops:
  0.0 7.6 %all-to-all-start = ((f32[8,144,128]{2,1,0:T(8,128)}), f32[8,144,128]{2,1,0:T(8,128)S(1)}, u32[]{:S(2)}, u32[]{:S(2)}) async-start(f32[8,144,128]{2,1,0:T(8,128)} %bitcast.23), calls=%async_computation | async-start | bytes 1179648 | tf_op jit(solution)/shard_map/all_to_all | solution.py:22
  8.3 0.0 copy-done.13
  8.3 0.2 copy.16
  8.5 0.1 reshape.25
  8.6 0.1 copy.17
  8.7 10.5 %all-to-all-done = f32[8,144,128]{2,1,0:T(8,128)S(1)} async-done(((f32[8,144,128]{2,1,0:T(8,128)}), f32[8,144,128]{2,1,0:T(8,128)S(1)}, u32[]{:S(2)}, u32[]{:S(2)}) %all-to-all-start) | async-done | bytes 589856 | tf_op jit(solution)/shard_map/all_to_all | solution.py:22
  19.2 0.0 copy-start.7
  19.2 0.0 copy-start.8
  19.2 0.0 copy-start.11
  19.2 0.0 copy-start.12
  19.2 26.9 %all-gather = f32[576,128]{1,0:T(8,128)S(1)} all-gather(f32[144,128]{1,0:T(8,128)S(1)} %dynamic-slice_bitcast_fusion.1), channel_id=2, replica_groups=mesh['z_far'=4,'z_near'=4,'y_lo'=2,'x'=4,'y_hi'=2,'core'=2] {'z_far'}, dimensions={0}, use_global_device_ids=true | all-gather | bytes 368640 | tf_op jit(solution)/shard_map/all_gather | solution.py:35
  46.2 20.0 %all_to_all.20 = f32[8,144,128]{2,1,0:T(8,128)S(1)} all-to-all(f32[8,144,128]{2,1,0:T(8,128)S(1)} %broadcast_in_dim.9), channel_id=1, replica_groups=mesh['z_far'=4,'z_near'=4,'y_lo'=2,'x'=4,'y_hi'=2,'core'=2] {'z_near','y..., dimensions={0} | all-to-all | bytes 1179648 | tf_op jit(solution)/shard_map/all_to_all | solution.py:28
  66.2 0.0 copy-done
  66.2 0.0 copy-done.7
  66.2 0.0 copy-done.8
  66.2 0.0 copy-done.11
  66.2 0.0 copy-done.12
  66.2 2.2 %shard_map.145 = f32[2304,128]{1,0:T(8,128)S(1)} custom-call(f32[2,6,96,128]{3,2,1,0:T(8,128)S(1)} %copy-done, f32[2,6,96,128]{3,2,1,0:T(8,128)S(1)} %bitcast.24, bf16[256,256]{1,0:T(8,128)(2,1)S(1)} %copy-done.8, bf16[256,256]{1,0:T(8,128)(2,1)S(1)} %copy-done.7, bf16[192,192]{1,0:T(8,128)(2,1)S(1)} %copy-done.12, bf16[192,192]{1,0:T(8,128)(2,1)S(1)} %copy-done.11), custom_call_target="tpu_custom_call" | custom-call | flops 792723456 | bytes 2768896 | tf_op jit(solution)/shard_map/pallas_call | solution.py:173
  68.4 0.0 copy-start.1
  68.5 0.0 copy-start.2
  68.5 0.0 copy-start.3
  68.5 0.0 copy-start.4
  68.5 28.0 %all_to_all.21 = f32[16,144,128]{2,1,0:T(8,128)S(1)} all-to-all(f32[16,144,128]{2,1,0:T(8,128)S(1)} %bitcast.22), channel_id=1, replica_groups=mesh['z_far'=4,'z_near'=4,'y_lo'=2,'x'=4,'y_hi'=2,'core'=2] {'x','y_hi',..., dimensions={0} | all-to-all | bytes 2359296 | tf_op jit(solution)/shard_map/all_to_all | solution.py:204
  96.5 0.0 copy-done.1
  96.5 1.8 %shard_map.146 = f32[2304,128]{1,0:T(8,128)S(1)} custom-call(f32[2304,128]{1,0:T(8,128)S(1)} %bitcast.18, f32[96,768]{1,0:T(8,128)S(1)} %bitcast.20, bf16[192,192]{1,0:T(8,128)(2,1)S(1)} %copy-done.4, bf16[192,192]{1,0:T(8,128)(2,1)S(1)} %copy-done.3, bf16[192,192]{1,0:T(8,128)(2,1)S(1)} %copy-done.2, bf16[192,192]{1,0:T(8,128)(2,1)S(1)} %copy-done.1), custom_call_target="tpu_custom_call" | custom-call | flops 679477248 | bytes 2949120 | tf_op jit(solution)/shard_map/pallas_call | solution.py:173
  98.2 0.0 copy-start.5
  98.3 0.0 copy-start.6
  98.3 0.0 copy-start.9
  98.3 0.0 copy-start.10
  98.3 21.9 %all_to_all.22 = f32[16,144,128]{2,1,0:T(8,128)S(1)} all-to-all(f32[16,144,128]{2,1,0:T(8,128)S(1)} %bitcast.19), channel_id=1, replica_groups=mesh['z_far'=4,'z_near'=4,'y_lo'=2,'x'=4,'y_hi'=2,'core'=2] {'x','y_hi',..., dimensions={0} | all-to-all | bytes 2359296 | tf_op jit(solution)/shard_map/all_to_all | solution.py:204
  120.2 0.0 copy-done.6
  120.3 2.5 %shard_map.147 = f32[2,6,96,128]{3,2,1,0:T(8,128)} custom-call(f32[2304,128]{1,0:T(8,128)S(1)} %bitcast.21, f32[2,6,96,128]{3,2,1,0:T(8,128)S(1)} %bitcast.25, bf16[192,192]{1,0:T(8,128)(2,1)S(1)} %copy-done.10, bf16[192,192]{1,0:T(8,128)(2,1)S(1)} %copy-done.9, bf16[256,256]{1,0:T(8,128)(2,1)S(1)} %copy-done.6, bf16[256,256]{1,0:T(8,128)(2,1)S(1)} %copy-done.5), custom_call_target="tpu_custom_call" | custom-call | flops 792723456 | bytes 2768896 | tf_op jit(solution)/shard_map/pallas_call | solution.py:173
  (11 shorter events, 0.1 us)
Async XLA Ops:
  0.0 8.3 %copy-start.13 = (f32[96,6,128]{2,0,1:T(8,128)S(1)}, f32[96,6,128]{2,0,1:T(8,128)}, u32[]{:S(2)}) copy-start(f32[96,6,128]{2,0,1:T(8,128)} %param.16) | copy-start | bytes 884740
  0.0 19.1 %all-to-all-start = ((f32[8,144,128]{2,1,0:T(8,128)}), f32[8,144,128]{2,1,0:T(8,128)S(1)}, u32[]{:S(2)}, u32[]{:S(2)}) async-start(f32[8,144,128]{2,1,0:T(8,128)} %bitcast.23), calls=%async_computation | async-start | bytes 1179648 | tf_op jit(solution)/shard_map/all_to_all | solution.py:22
  19.2 47.0 %copy-start = (f32[2,6,96,128]{3,2,1,0:T(8,128)S(1)}, f32[2,6,96,128]{3,2,1,0:T(8,128)}, u32[]{:S(2)}) copy-start(f32[2,6,96,128]{3,2,1,0:T(8,128)} %orbitals.1) | copy-start | bytes 1769476
  19.2 47.0 %copy-start.7 = (bf16[256,256]{1,0:T(8,128)(2,1)S(1)}, bf16[256,256]{1,0:T(8,128)(2,1)}, u32[]{:S(2)}) copy-start(bf16[256,256]{1,0:T(8,128)(2,1)} %constant.60.clone.z_low) | copy-start | bytes 393220
  19.2 47.0 %copy-start.8 = (bf16[256,256]{1,0:T(8,128)(2,1)S(1)}, bf16[256,256]{1,0:T(8,128)(2,1)}, u32[]{:S(2)}) copy-start(bf16[256,256]{1,0:T(8,128)(2,1)} %constant.59.clone.z_up) | copy-start | bytes 393220
  19.2 47.0 %copy-start.11 = (bf16[192,192]{1,0:T(8,128)(2,1)S(1)}, bf16[192,192]{1,0:T(8,128)(2,1)}, u32[]{:S(2)}) copy-start(bf16[192,192]{1,0:T(8,128)(2,1)} %constant.62.clone.y_low) | copy-start | bytes 221188
  19.2 47.0 %copy-start.12 = (bf16[192,192]{1,0:T(8,128)(2,1)S(1)}, bf16[192,192]{1,0:T(8,128)(2,1)}, u32[]{:S(2)}) copy-start(bf16[192,192]{1,0:T(8,128)(2,1)} %constant.61.clone.y_up) | copy-start | bytes 221188
  68.4 28.0 %copy-start.1 = (bf16[192,192]{1,0:T(8,128)(2,1)S(1)}, bf16[192,192]{1,0:T(8,128)(2,1)}, u32[]{:S(2)}) copy-start(bf16[192,192]{1,0:T(8,128)(2,1)} %constant.66.clone.i_low) | copy-start | bytes 221188
  68.5 28.0 %copy-start.2 = (bf16[192,192]{1,0:T(8,128)(2,1)S(1)}, bf16[192,192]{1,0:T(8,128)(2,1)}, u32[]{:S(2)}) copy-start(bf16[192,192]{1,0:T(8,128)(2,1)} %constant.65.clone.i_up) | copy-start | bytes 221188
  68.5 28.0 %copy-start.3 = (bf16[192,192]{1,0:T(8,128)(2,1)S(1)}, bf16[192,192]{1,0:T(8,128)(2,1)}, u32[]{:S(2)}) copy-start(bf16[192,192]{1,0:T(8,128)(2,1)} %constant.64.clone.f_low) | copy-start | bytes 221188
  68.5 28.0 %copy-start.4 = (bf16[192,192]{1,0:T(8,128)(2,1)S(1)}, bf16[192,192]{1,0:T(8,128)(2,1)}, u32[]{:S(2)}) copy-start(bf16[192,192]{1,0:T(8,128)(2,1)} %constant.63.clone.f_up) | copy-start | bytes 221188
  98.2 22.0 %copy-start.5 = (bf16[256,256]{1,0:T(8,128)(2,1)S(1)}, bf16[256,256]{1,0:T(8,128)(2,1)}, u32[]{:S(2)}) copy-start(bf16[256,256]{1,0:T(8,128)(2,1)} %constant.70.clone.z_low) | copy-start | bytes 393220
  98.3 22.0 %copy-start.6 = (bf16[256,256]{1,0:T(8,128)(2,1)S(1)}, bf16[256,256]{1,0:T(8,128)(2,1)}, u32[]{:S(2)}) copy-start(bf16[256,256]{1,0:T(8,128)(2,1)} %constant.69.clone.z_up) | copy-start | bytes 393220
  98.3 22.0 %copy-start.9 = (bf16[192,192]{1,0:T(8,128)(2,1)S(1)}, bf16[192,192]{1,0:T(8,128)(2,1)}, u32[]{:S(2)}) copy-start(bf16[192,192]{1,0:T(8,128)(2,1)} %constant.68.clone.y_low) | copy-start | bytes 221188
  98.3 22.0 %copy-start.10 = (bf16[192,192]{1,0:T(8,128)(2,1)S(1)}, bf16[192,192]{1,0:T(8,128)(2,1)}, u32[]{:S(2)}) copy-start(bf16[192,192]{1,0:T(8,128)(2,1)} %constant.67.clone.y_up) | copy-start | bytes 221188

commit v4 on v3

--- a/solution.py
+++ b/solution.py
@@ -30,11 +30,13 @@
 
 def broadcast(block, holder, aside):
     members = lax.axis_size(near_axes)
-    piece = pieces_of(block, near_axes, holder % members)
+    flip = near_axes[::-1]
+    place = (holder % 2) * (members // 2) + (holder % members) // 2
+    piece = pieces_of(block, flip, place)
     piece, aside = lax.optimization_barrier((piece, aside))
     everywhere = lax.all_gather(piece, far_axis, axis=0)
     piece = lax.dynamic_index_in_dim(everywhere, holder // members, 0, keepdims=False)
-    return copies_of(piece, near_axes).reshape(block.shape), aside
+    return copies_of(piece, flip).reshape(block.shape), aside
 
 
 def wave(length, forward):

time: 123 us -> 122 us (level)
    all_to_all x1, blocking collectives: 20 us -> 17.3 us  [copies_of(): return lax.all_to_all(copies, axes, 0, 0, tiled=True)]
    all_to_all x2, blocking collectives: 49.9 us -> 52 us  [exchange(): return lax.all_to_all(columns, grid_axes, 0, 0, tiled=True).reshape(shape)]
where the time goes in v4:
time: 122 us
  blocking collectives  96.2 us (79%)
  waiting for transfers between devices  10.3 us (8%)
  starting transfers between devices  7.59 us (6%)
  Pallas kernels  6.51 us (5%)
    all_to_all x2, blocking collectives, exchange(): return lax.all_to_all(columns, grid_axes, 0, 0, tiled=True).reshape(shape)  52 us
    all_gather x1, blocking collectives, broadcast(): everywhere = lax.all_gather(piece, far_axis, axis=0)  26.8 us
    all_to_all x1, blocking collectives, copies_of(): return lax.all_to_all(copies, axes, 0, 0, tiled=True)  17.3 us
    all_to_all x1, waiting for transfers between devices, pieces_of(): received = lax.all_to_all(pieces, axes, 0, 0, tiled=True)  10.3 us
    all_to_all x1, starting transfers between devices, pieces_of(): received = lax.all_to_all(pieces, axes, 0, 0, tiled=True)  7.59 us
    pallas_call x3, Pallas kernels, on_device(): pl.pallas_call(body, out_shape=jax.ShapeDtypeStruct(shape, jnp.float32),...  6.51 us
  transfers between devices with their start and end apart: 1, of which 1 were waited for; matrix products, arithmetic and copies ran while one was open for 0% of the time, Pallas kernels for 0%

profile of v4, /device:TPU:1, one launch (start us, length us, event | category | flops | bytes accessed | tf_op | source)
XLA Modules:
  0.0 122.1 jit_solution(1775955595706258599)
XLA Ops:
  0.0 7.6 %all-to-all-start = ((f32[8,144,128]{2,1,0:T(8,128)}), f32[8,144,128]{2,1,0:T(8,128)S(1)}, u32[]{:S(2)}, u32[]{:S(2)}) async-start(f32[8,144,128]{2,1,0:T(8,128)} %bitcast.23), calls=%async_computation | async-start | bytes 1179648 | tf_op jit(solution)/shard_map/all_to_all | solution.py:22
  8.3 0.0 copy-done.13
  8.3 0.2 copy.16
  8.5 0.1 reshape.25
  8.6 0.1 copy.17
  8.7 10.3 %all-to-all-done = f32[8,144,128]{2,1,0:T(8,128)S(1)} async-done(((f32[8,144,128]{2,1,0:T(8,128)}), f32[8,144,128]{2,1,0:T(8,128)S(1)}, u32[]{:S(2)}, u32[]{:S(2)}) %all-to-all-start) | async-done | bytes 589856 | tf_op jit(solution)/shard_map/all_to_all | solution.py:22
  19.1 0.0 copy-start.7
  19.1 0.0 copy-start.8
  19.1 0.0 copy-start.11
  19.1 0.0 copy-start.12
  19.1 26.8 %all-gather = f32[576,128]{1,0:T(8,128)S(1)} all-gather(f32[144,128]{1,0:T(8,128)S(1)} %dynamic-slice_bitcast_fusion.1), channel_id=2, replica_groups=mesh['z_far'=4,'z_near'=4,'y_lo'=2,'x'=4,'y_hi'=2,'core'=2] {'z_far'}, dimensions={0}, use_global_device_ids=true | all-gather | bytes 368640 | tf_op jit(solution)/shard_map/all_gather | solution.py:37
  46.0 17.3 %all_to_all.20 = f32[8,144,128]{2,1,0:T(8,128)S(1)} all-to-all(f32[8,144,128]{2,1,0:T(8,128)S(1)} %broadcast_in_dim.9), channel_id=1, replica_groups=mesh['z_far'=4,'z_near'=4,'y_lo'=2,'x'=4,'y_hi'=2,'core'=2] {'y_lo','z_n..., dimensions={0} | all-to-all | bytes 1179648 | tf_op jit(solution)/shard_map/all_to_all | solution.py:28
  63.3 0.0 copy-done
  63.3 0.0 copy-done.7
  63.3 0.0 copy-done.8
  63.4 0.0 copy-done.11
  63.4 0.0 copy-done.12
  63.4 2.2 %shard_map.145 = f32[2304,128]{1,0:T(8,128)S(1)} custom-call(f32[2,6,96,128]{3,2,1,0:T(8,128)S(1)} %copy-done, f32[2,6,96,128]{3,2,1,0:T(8,128)S(1)} %bitcast.24, bf16[256,256]{1,0:T(8,128)(2,1)S(1)} %copy-done.8, bf16[256,256]{1,0:T(8,128)(2,1)S(1)} %copy-done.7, bf16[192,192]{1,0:T(8,128)(2,1)S(1)} %copy-done.12, bf16[192,192]{1,0:T(8,128)(2,1)S(1)} %copy-done.11), custom_call_target="tpu_custom_call" | custom-call | flops 792723456 | bytes 2768896 | tf_op jit(solution)/shard_map/pallas_call | solution.py:175
  65.6 0.0 copy-start.1
  65.6 0.0 copy-start.2
  65.6 0.0 copy-start.3
  65.6 0.0 copy-start.4
  65.6 30.1 %all_to_all.21 = f32[16,144,128]{2,1,0:T(8,128)S(1)} all-to-all(f32[16,144,128]{2,1,0:T(8,128)S(1)} %bitcast.22), channel_id=1, replica_groups=mesh['z_far'=4,'z_near'=4,'y_lo'=2,'x'=4,'y_hi'=2,'core'=2] {'x','y_hi',..., dimensions={0} | all-to-all | bytes 2359296 | tf_op jit(solution)/shard_map/all_to_all | solution.py:206
  95.7 0.0 copy-done.1
  95.8 1.8 %shard_map.146 = f32[2304,128]{1,0:T(8,128)S(1)} custom-call(f32[2304,128]{1,0:T(8,128)S(1)} %bitcast.18, f32[96,768]{1,0:T(8,128)S(1)} %bitcast.20, bf16[192,192]{1,0:T(8,128)(2,1)S(1)} %copy-done.4, bf16[192,192]{1,0:T(8,128)(2,1)S(1)} %copy-done.3, bf16[192,192]{1,0:T(8,128)(2,1)S(1)} %copy-done.2, bf16[192,192]{1,0:T(8,128)(2,1)S(1)} %copy-done.1), custom_call_target="tpu_custom_call" | custom-call | flops 679477248 | bytes 2949120 | tf_op jit(solution)/shard_map/pallas_call | solution.py:175
  97.5 0.0 copy-start.5
  97.5 0.0 copy-start.6
  97.5 0.0 copy-start.9
  97.6 0.0 copy-start.10
  97.6 21.9 %all_to_all.22 = f32[16,144,128]{2,1,0:T(8,128)S(1)} all-to-all(f32[16,144,128]{2,1,0:T(8,128)S(1)} %bitcast.19), channel_id=1, replica_groups=mesh['z_far'=4,'z_near'=4,'y_lo'=2,'x'=4,'y_hi'=2,'core'=2] {'x','y_hi',..., dimensions={0} | all-to-all | bytes 2359296 | tf_op jit(solution)/shard_map/all_to_all | solution.py:206
  119.5 0.0 copy-done.10
  119.5 2.5 %shard_map.147 = f32[2,6,96,128]{3,2,1,0:T(8,128)} custom-call(f32[2304,128]{1,0:T(8,128)S(1)} %bitcast.21, f32[2,6,96,128]{3,2,1,0:T(8,128)S(1)} %bitcast.25, bf16[192,192]{1,0:T(8,128)(2,1)S(1)} %copy-done.10, bf16[192,192]{1,0:T(8,128)(2,1)S(1)} %copy-done.9, bf16[256,256]{1,0:T(8,128)(2,1)S(1)} %copy-done.6, bf16[256,256]{1,0:T(8,128)(2,1)S(1)} %copy-done.5), custom_call_target="tpu_custom_call" | custom-call | flops 792723456 | bytes 2768896 | tf_op jit(solution)/shard_map/pallas_call | solution.py:175
  (11 shorter events, 0.1 us)
Async XLA Ops:
  0.0 8.3 %copy-start.13 = (f32[96,6,128]{2,0,1:T(8,128)S(1)}, f32[96,6,128]{2,0,1:T(8,128)}, u32[]{:S(2)}) copy-start(f32[96,6,128]{2,0,1:T(8,128)} %param.16) | copy-start | bytes 884740
  0.0 19.1 %all-to-all-start = ((f32[8,144,128]{2,1,0:T(8,128)}), f32[8,144,128]{2,1,0:T(8,128)S(1)}, u32[]{:S(2)}, u32[]{:S(2)}) async-start(f32[8,144,128]{2,1,0:T(8,128)} %bitcast.23), calls=%async_computation | async-start | bytes 1179648 | tf_op jit(solution)/shard_map/all_to_all | solution.py:22
  19.1 44.3 %copy-start = (f32[2,6,96,128]{3,2,1,0:T(8,128)S(1)}, f32[2,6,96,128]{3,2,1,0:T(8,128)}, u32[]{:S(2)}) copy-start(f32[2,6,96,128]{3,2,1,0:T(8,128)} %orbitals.1) | copy-start | bytes 1769476
  19.1 44.3 %copy-start.7 = (bf16[256,256]{1,0:T(8,128)(2,1)S(1)}, bf16[256,256]{1,0:T(8,128)(2,1)}, u32[]{:S(2)}) copy-start(bf16[256,256]{1,0:T(8,128)(2,1)} %constant.78.clone.z_low) | copy-start | bytes 393220
  19.1 44.3 %copy-start.8 = (bf16[256,256]{1,0:T(8,128)(2,1)S(1)}, bf16[256,256]{1,0:T(8,128)(2,1)}, u32[]{:S(2)}) copy-start(bf16[256,256]{1,0:T(8,128)(2,1)} %constant.77.clone.z_up) | copy-start | bytes 393220
  19.1 44.3 %copy-start.11 = (bf16[192,192]{1,0:T(8,128)(2,1)S(1)}, bf16[192,192]{1,0:T(8,128)(2,1)}, u32[]{:S(2)}) copy-start(bf16[192,192]{1,0:T(8,128)(2,1)} %constant.80.clone.y_low) | copy-start | bytes 221188
  19.1 44.3 %copy-start.12 = (bf16[192,192]{1,0:T(8,128)(2,1)S(1)}, bf16[192,192]{1,0:T(8,128)(2,1)}, u32[]{:S(2)}) copy-start(bf16[192,192]{1,0:T(8,128)(2,1)} %constant.79.clone.y_up) | copy-start | bytes 221188
  65.6 30.1 %copy-start.1 = (bf16[192,192]{1,0:T(8,128)(2,1)S(1)}, bf16[192,192]{1,0:T(8,128)(2,1)}, u32[]{:S(2)}) copy-start(bf16[192,192]{1,0:T(8,128)(2,1)} %constant.84.clone.i_low) | copy-start | bytes 221188
  65.6 30.1 %copy-start.2 = (bf16[192,192]{1,0:T(8,128)(2,1)S(1)}, bf16[192,192]{1,0:T(8,128)(2,1)}, u32[]{:S(2)}) copy-start(bf16[192,192]{1,0:T(8,128)(2,1)} %constant.83.clone.i_up) | copy-start | bytes 221188
  65.6 30.1 %copy-start.3 = (bf16[192,192]{1,0:T(8,128)(2,1)S(1)}, bf16[192,192]{1,0:T(8,128)(2,1)}, u32[]{:S(2)}) copy-start(bf16[192,192]{1,0:T(8,128)(2,1)} %constant.82.clone.f_low) | copy-start | bytes 221188
  65.6 30.1 %copy-start.4 = (bf16[192,192]{1,0:T(8,128)(2,1)S(1)}, bf16[192,192]{1,0:T(8,128)(2,1)}, u32[]{:S(2)}) copy-start(bf16[192,192]{1,0:T(8,128)(2,1)} %constant.81.clone.f_up) | copy-start | bytes 221188
  97.5 22.0 %copy-start.5 = (bf16[256,256]{1,0:T(8,128)(2,1)S(1)}, bf16[256,256]{1,0:T(8,128)(2,1)}, u32[]{:S(2)}) copy-start(bf16[256,256]{1,0:T(8,128)(2,1)} %constant.88.clone.z_low) | copy-start | bytes 393220
  97.5 22.0 %copy-start.6 = (bf16[256,256]{1,0:T(8,128)(2,1)S(1)}, bf16[256,256]{1,0:T(8,128)(2,1)}, u32[]{:S(2)}) copy-start(bf16[256,256]{1,0:T(8,128)(2,1)} %constant.87.clone.z_up) | copy-start | bytes 393220
  97.5 22.0 %copy-start.9 = (bf16[192,192]{1,0:T(8,128)(2,1)S(1)}, bf16[192,192]{1,0:T(8,128)(2,1)}, u32[]{:S(2)}) copy-start(bf16[192,192]{1,0:T(8,128)(2,1)} %constant.86.clone.y_low) | copy-start | bytes 221188
  97.6 22.0 %copy-start.10 = (bf16[192,192]{1,0:T(8,128)(2,1)S(1)}, bf16[192,192]{1,0:T(8,128)(2,1)}, u32[]{:S(2)}) copy-start(bf16[192,192]{1,0:T(8,128)(2,1)} %constant.85.clone.y_up) | copy-start | bytes 221188

commit v5 on v4

--- a/solution.py
+++ b/solution.py
@@ -28,14 +28,32 @@
     return lax.all_to_all(copies, axes, 0, 0, tiled=True)
 
 
+def far_copies(piece, source):
+    count = lax.axis_size(far_axis)
+    mine = lax.axis_index(far_axis)
+    order = sorted(range(count), key=lambda place: min(place, count - place))
+
+    def sent_by(first):
+        def send(piece):
+            result = piece
+            for target in order:
+                if target != first:
+                    got = lax.ppermute(piece, far_axis, [(first, target)])
+                    result = jnp.where(mine == target, got, result)
+            return result
+
+        return send
+
+    return lax.switch(source, [sent_by(first) for first in range(count)], piece)
+
+
 def broadcast(block, holder, aside):
     members = lax.axis_size(near_axes)
     flip = near_axes[::-1]
     place = (holder % 2) * (members // 2) + (holder % members) // 2
     piece = pieces_of(block, flip, place)
     piece, aside = lax.optimization_barrier((piece, aside))
-    everywhere = lax.all_gather(piece, far_axis, axis=0)
-    piece = lax.dynamic_index_in_dim(everywhere, holder // members, 0, keepdims=False)
+    piece = far_copies(piece, holder // members)
     return copies_of(piece, flip).reshape(block.shape), aside
 
 

time: 122 us -> 117 us (0.959)
  blocking collectives: 96.2 us -> 67.7 us
  starting transfers between devices: 7.59 us -> 27.8 us
  waiting for transfers between devices: 10.3 us -> 13.5 us
    all_gather x1 -> x0, blocking collectives: 26.8 us -> none  [broadcast(): everywhere = lax.all_gather(piece, far_axis, axis=0)]
    ppermute x0 -> x3, starting transfers between devices: none -> 20.2 us  [send(): got = lax.ppermute(piece, far_axis, [(first, target)])]
    ppermute x0 -> x3, waiting for transfers between devices: none -> 3.11 us  [send(): got = lax.ppermute(piece, far_axis, [(first, target)])]
    all_to_all x2, blocking collectives: 52 us -> 49.5 us  [exchange(): return lax.all_to_all(columns, grid_axes, 0, 0, tiled=True).reshape(shape)]
  transfers between devices with their start and end apart: 1 -> 4, of which waited for: 1 -> 2; matrix products, arithmetic and copies ran while one was open for 0% -> 0% of each run, Pallas kernels for 0% -> 0%
where the time goes in v5:
time: 117 us
  blocking collectives  67.7 us (58%)
  starting transfers between devices  27.8 us (24%)
  waiting for transfers between devices  13.5 us (12%)
  Pallas kernels  6.51 us (6%)
    all_to_all x2, blocking collectives, exchange(): return lax.all_to_all(columns, grid_axes, 0, 0, tiled=True).reshape(shape)  49.5 us
    ppermute x3, starting transfers between devices, send(): got = lax.ppermute(piece, far_axis, [(first, target)])  20.2 us
    all_to_all x1, blocking collectives, copies_of(): return lax.all_to_all(copies, axes, 0, 0, tiled=True)  18.2 us
    all_to_all x1, waiting for transfers between devices, pieces_of(): received = lax.all_to_all(pieces, axes, 0, 0, tiled=True)  10.4 us
    all_to_all x1, starting transfers between devices, pieces_of(): received = lax.all_to_all(pieces, axes, 0, 0, tiled=True)  7.59 us
    pallas_call x3, Pallas kernels, on_device(): pl.pallas_call(body, out_shape=jax.ShapeDtypeStruct(shape, jnp.float32),...  6.51 us
    ppermute x3, waiting for transfers between devices, send(): got = lax.ppermute(piece, far_axis, [(first, target)])  3.11 us
  transfers between devices with their start and end apart: 4, of which 2 were waited for; matrix products, arithmetic and copies ran while one was open for 0% of the time, Pallas kernels for 0%

profile of v5, /device:TPU:1, one launch (start us, length us, event | category | flops | bytes accessed | tf_op | source)
XLA Modules:
  0.0 116.9 jit_solution(5942309373708540746)
XLA Ops:
  0.0 7.6 %all-to-all-start = ((f32[8,144,128]{2,1,0:T(8,128)}), f32[8,144,128]{2,1,0:T(8,128)S(1)}, u32[]{:S(2)}, u32[]{:S(2)}) async-start(f32[8,144,128]{2,1,0:T(8,128)} %bitcast.20), calls=%async_computation | async-start | bytes 1179648 | tf_op jit(solution)/shard_map/all_to_all | solution.py:22
  8.3 0.2 copy.16
  8.5 0.1 reshape.26
  8.6 0.1 copy.17
  8.7 10.4 %all-to-all-done = f32[8,144,128]{2,1,0:T(8,128)S(1)} async-done(((f32[8,144,128]{2,1,0:T(8,128)}), f32[8,144,128]{2,1,0:T(8,128)S(1)}, u32[]{:S(2)}, u32[]{:S(2)}) %all-to-all-start) | async-done | bytes 589856 | tf_op jit(solution)/shard_map/all_to_all | solution.py:22
  19.1 0.0 copy-start.7
  19.1 0.0 copy-start.8
  19.1 0.0 copy-start.11
  19.1 0.0 copy-start.12
  19.1 23.3 %conditional.1 = (f32[144,128]{1,0:T(8,128)}, f32[144,128]{1,0:T(8,128)}, s32[]{:T(128)}, s32[]{:T(128)}, s32[]{:T(128)}, /*index=5*/f32[144,128]{1,0:T(8,128)},...) conditional(s32[]{:T(128)} %clamp.3, ...), branch_computations={%region_0.1_spmd, %region_1.2_spmd, %region_2.3_spmd, %region_3.4_... | conditional | bytes 884960 | solution.py:47
  19.1 13.7 %collective-permute-start.2 = (f32[144,128]{1,0:T(8,128)S(1)}, f32[144,128]{1,0:T(8,128)}, u32[]{:S(2)}, u32[]{:S(2)}) collective-permute-start(f32[144,128]{1,0:T(8,128)S(1)} %get-tuple-element.67), channel_id=1, source_target_pairs={{0,128},{1,129},{2,130},{3,131},{4,132},{5,133},{6,134},{7,135},{8... | collective-permute-start | bytes 221192 | tf_op jit(solution)/shard_map/cond/branch_0_fun/ppermute | solution.py:41
  32.8 2.2 %collective-permute-start.1 = (f32[144,128]{1,0:T(8,128)S(1)}, f32[144,128]{1,0:T(8,128)}, u32[]{:S(2)}, u32[]{:S(2)}) collective-permute-start(f32[144,128]{1,0:T(8,128)S(1)} %get-tuple-element.67), channel_id=1, source_target_pairs={{0,384},{1,385},{2,386},{3,387},{4,388},{5,389},{6,390},{7,391},{8... | collective-permute-start | bytes 221192 | tf_op jit(solution)/shard_map/cond/branch_0_fun/ppermute | solution.py:41
  35.1 4.3 %collective-permute-start = (f32[144,128]{1,0:T(8,128)S(1)}, f32[144,128]{1,0:T(8,128)}, u32[]{:S(2)}, u32[]{:S(2)}) collective-permute-start(f32[144,128]{1,0:T(8,128)S(1)} %get-tuple-element.67), channel_id=1, source_target_pairs={{0,256},{1,257},{2,258},{3,259},{4,260},{5,261},{6,262},{7,263},{8... | collective-permute-start | bytes 221192 | tf_op jit(solution)/shard_map/cond/branch_0_fun/ppermute | solution.py:41
  39.3 0.0 collective-permute-done.2
  39.3 3.1 %collective-permute-done.1 = f32[144,128]{1,0:T(8,128)} collective-permute-done((f32[144,128]{1,0:T(8,128)S(1)}, f32[144,128]{1,0:T(8,128)}, u32[]{:S(2)}, u32[]{:S(2)}) %collective-permute-start.1) | collective-permute-done | bytes 73760 | tf_op jit(solution)/shard_map/cond/branch_0_fun/ppermute | solution.py:41
  42.4 0.0 collective-permute-done
  42.5 18.2 %all_to_all.20 = f32[8,144,128]{2,1,0:T(8,128)S(1)} all-to-all(f32[8,144,128]{2,1,0:T(8,128)S(1)} %broadcast_in_dim.2), channel_id=1, replica_groups=mesh['z_far'=4,'z_near'=4,'y_lo'=2,'x'=4,'y_hi'=2,'core'=2] {'y_lo','z_n..., dimensions={0} | all-to-all | bytes 1179648 | tf_op jit(solution)/shard_map/all_to_all | solution.py:28
  60.7 0.0 copy-done.8
  60.7 2.2 %shard_map.145 = f32[2304,128]{1,0:T(8,128)S(1)} custom-call(f32[2,6,96,128]{3,2,1,0:T(8,128)S(1)} %copy-done, f32[2,6,96,128]{3,2,1,0:T(8,128)S(1)} %bitcast.21, bf16[256,256]{1,0:T(8,128)(2,1)S(1)} %copy-done.8, bf16[256,256]{1,0:T(8,128)(2,1)S(1)} %copy-done.7, bf16[192,192]{1,0:T(8,128)(2,1)S(1)} %copy-done.12, bf16[192,192]{1,0:T(8,128)(2,1)S(1)} %copy-done.11), custom_call_target="tpu_custom_call" | custom-call | flops 792723456 | bytes 2768896 | tf_op jit(solution)/shard_map/pallas_call | solution.py:193
  62.9 0.0 copy-start.1
  62.9 0.0 copy-start.2
  62.9 0.0 copy-start.3
  62.9 0.0 copy-start.4
  63.0 27.6 %all_to_all.21 = f32[16,144,128]{2,1,0:T(8,128)S(1)} all-to-all(f32[16,144,128]{2,1,0:T(8,128)S(1)} %bitcast.19), channel_id=1, replica_groups=mesh['z_far'=4,'z_near'=4,'y_lo'=2,'x'=4,'y_hi'=2,'core'=2] {'x','y_hi',..., dimensions={0} | all-to-all | bytes 2359296 | tf_op jit(solution)/shard_map/all_to_all | solution.py:224
  90.6 0.0 copy-done.3
  90.6 1.8 %shard_map.146 = f32[2304,128]{1,0:T(8,128)S(1)} custom-call(f32[2304,128]{1,0:T(8,128)S(1)} %bitcast.15, f32[96,768]{1,0:T(8,128)S(1)} %bitcast.17, bf16[192,192]{1,0:T(8,128)(2,1)S(1)} %copy-done.4, bf16[192,192]{1,0:T(8,128)(2,1)S(1)} %copy-done.3, bf16[192,192]{1,0:T(8,128)(2,1)S(1)} %copy-done.2, bf16[192,192]{1,0:T(8,128)(2,1)S(1)} %copy-done.1), custom_call_target="tpu_custom_call" | custom-call | flops 679477248 | bytes 2949120 | tf_op jit(solution)/shard_map/pallas_call | solution.py:193
  92.3 0.0 copy-start.5
  92.4 0.0 copy-start.6
  92.4 0.0 copy-start.9
  92.4 0.0 copy-start.10
  92.4 21.9 %all_to_all.22 = f32[16,144,128]{2,1,0:T(8,128)S(1)} all-to-all(f32[16,144,128]{2,1,0:T(8,128)S(1)} %bitcast.16), channel_id=1, replica_groups=mesh['z_far'=4,'z_near'=4,'y_lo'=2,'x'=4,'y_hi'=2,'core'=2] {'x','y_hi',..., dimensions={0} | all-to-all | bytes 2359296 | tf_op jit(solution)/shard_map/all_to_all | solution.py:224
  114.4 2.5 %shard_map.147 = f32[2,6,96,128]{3,2,1,0:T(8,128)} custom-call(f32[2304,128]{1,0:T(8,128)S(1)} %bitcast.18, f32[2,6,96,128]{3,2,1,0:T(8,128)S(1)} %bitcast.22, bf16[192,192]{1,0:T(8,128)(2,1)S(1)} %copy-done.10, bf16[192,192]{1,0:T(8,128)(2,1)S(1)} %copy-done.9, bf16[256,256]{1,0:T(8,128)(2,1)S(1)} %copy-done.6, bf16[256,256]{1,0:T(8,128)(2,1)S(1)} %copy-done.5), custom_call_target="tpu_custom_call" | custom-call | flops 792723456 | bytes 2768896 | tf_op jit(solution)/shard_map/pallas_call | solution.py:193
  (17 shorter events, 0.1 us)
Async XLA Ops:
  0.0 8.3 %copy-start.13 = (f32[96,6,128]{2,0,1:T(8,128)S(1)}, f32[96,6,128]{2,0,1:T(8,128)}, u32[]{:S(2)}) copy-start(f32[96,6,128]{2,0,1:T(8,128)} %param.20) | copy-start | bytes 884740
  0.0 19.1 %all-to-all-start = ((f32[8,144,128]{2,1,0:T(8,128)}), f32[8,144,128]{2,1,0:T(8,128)S(1)}, u32[]{:S(2)}, u32[]{:S(2)}) async-start(f32[8,144,128]{2,1,0:T(8,128)} %bitcast.20), calls=%async_computation | async-start | bytes 1179648 | tf_op jit(solution)/shard_map/all_to_all | solution.py:22
  19.1 41.6 %copy-start = (f32[2,6,96,128]{3,2,1,0:T(8,128)S(1)}, f32[2,6,96,128]{3,2,1,0:T(8,128)}, u32[]{:S(2)}) copy-start(f32[2,6,96,128]{3,2,1,0:T(8,128)} %orbitals.1) | copy-start | bytes 1769476
  19.1 41.6 %copy-start.7 = (bf16[256,256]{1,0:T(8,128)(2,1)S(1)}, bf16[256,256]{1,0:T(8,128)(2,1)}, u32[]{:S(2)}) copy-start(bf16[256,256]{1,0:T(8,128)(2,1)} %constant.106.clone.z_low) | copy-start | bytes 393220
  19.1 41.6 %copy-start.8 = (bf16[256,256]{1,0:T(8,128)(2,1)S(1)}, bf16[256,256]{1,0:T(8,128)(2,1)}, u32[]{:S(2)}) copy-start(bf16[256,256]{1,0:T(8,128)(2,1)} %constant.105.clone.z_up) | copy-start | bytes 393220
  19.1 41.6 %copy-start.11 = (bf16[192,192]{1,0:T(8,128)(2,1)S(1)}, bf16[192,192]{1,0:T(8,128)(2,1)}, u32[]{:S(2)}) copy-start(bf16[192,192]{1,0:T(8,128)(2,1)} %constant.108.clone.y_low) | copy-start | bytes 221188
  19.1 41.6 %copy-start.12 = (bf16[192,192]{1,0:T(8,128)(2,1)S(1)}, bf16[192,192]{1,0:T(8,128)(2,1)}, u32[]{:S(2)}) copy-start(bf16[192,192]{1,0:T(8,128)(2,1)} %constant.107.clone.y_up) | copy-start | bytes 221188
  19.1 20.2 %collective-permute-start.2 = (f32[144,128]{1,0:T(8,128)S(1)}, f32[144,128]{1,0:T(8,128)}, u32[]{:S(2)}, u32[]{:S(2)}) collective-permute-start(f32[144,128]{1,0:T(8,128)S(1)} %get-tuple-element.67), channel_id=1, source_target_pairs={{0,128},{1,129},{2,130},{3,131},{4,132},{5,133},{6,134},{7,135},{8... | collective-permute-start | bytes 221192 | tf_op jit(solution)/shard_map/cond/branch_0_fun/ppermute | solution.py:41
  32.8 9.6 %collective-permute-start.1 = (f32[144,128]{1,0:T(8,128)S(1)}, f32[144,128]{1,0:T(8,128)}, u32[]{:S(2)}, u32[]{:S(2)}) collective-permute-start(f32[144,128]{1,0:T(8,128)S(1)} %get-tuple-element.67), channel_id=1, source_target_pairs={{0,384},{1,385},{2,386},{3,387},{4,388},{5,389},{6,390},{7,391},{8... | collective-permute-start | bytes 221192 | tf_op jit(solution)/shard_map/cond/branch_0_fun/ppermute | solution.py:41
  35.1 7.4 %collective-permute-start = (f32[144,128]{1,0:T(8,128)S(1)}, f32[144,128]{1,0:T(8,128)}, u32[]{:S(2)}, u32[]{:S(2)}) collective-permute-start(f32[144,128]{1,0:T(8,128)S(1)} %get-tuple-element.67), channel_id=1, source_target_pairs={{0,256},{1,257},{2,258},{3,259},{4,260},{5,261},{6,262},{7,263},{8... | collective-permute-start | bytes 221192 | tf_op jit(solution)/shard_map/cond/branch_0_fun/ppermute | solution.py:41
  62.9 27.7 %copy-start.1 = (bf16[192,192]{1,0:T(8,128)(2,1)S(1)}, bf16[192,192]{1,0:T(8,128)(2,1)}, u32[]{:S(2)}) copy-start(bf16[192,192]{1,0:T(8,128)(2,1)} %constant.112.clone.i_low) | copy-start | bytes 221188
  62.9 27.6 %copy-start.2 = (bf16[192,192]{1,0:T(8,128)(2,1)S(1)}, bf16[192,192]{1,0:T(8,128)(2,1)}, u32[]{:S(2)}) copy-start(bf16[192,192]{1,0:T(8,128)(2,1)} %constant.111.clone.i_up) | copy-start | bytes 221188
  62.9 27.6 %copy-start.3 = (bf16[192,192]{1,0:T(8,128)(2,1)S(1)}, bf16[192,192]{1,0:T(8,128)(2,1)}, u32[]{:S(2)}) copy-start(bf16[192,192]{1,0:T(8,128)(2,1)} %constant.110.clone.f_low) | copy-start | bytes 221188
  62.9 27.6 %copy-start.4 = (bf16[192,192]{1,0:T(8,128)(2,1)S(1)}, bf16[192,192]{1,0:T(8,128)(2,1)}, u32[]{:S(2)}) copy-start(bf16[192,192]{1,0:T(8,128)(2,1)} %constant.109.clone.f_up) | copy-start | bytes 221188
  92.3 22.0 %copy-start.5 = (bf16[256,256]{1,0:T(8,128)(2,1)S(1)}, bf16[256,256]{1,0:T(8,128)(2,1)}, u32[]{:S(2)}) copy-start(bf16[256,256]{1,0:T(8,128)(2,1)} %constant.116.clone.z_low) | copy-start | bytes 393220
  92.4 22.0 %copy-start.6 = (bf16[256,256]{1,0:T(8,128)(2,1)S(1)}, bf16[256,256]{1,0:T(8,128)(2,1)}, u32[]{:S(2)}) copy-start(bf16[256,256]{1,0:T(8,128)(2,1)} %constant.115.clone.z_up) | copy-start | bytes 393220
  92.4 22.0 %copy-start.9 = (bf16[192,192]{1,0:T(8,128)(2,1)S(1)}, bf16[192,192]{1,0:T(8,128)(2,1)}, u32[]{:S(2)}) copy-start(bf16[192,192]{1,0:T(8,128)(2,1)} %constant.114.clone.y_low) | copy-start | bytes 221188
  92.4 22.0 %copy-start.10 = (bf16[192,192]{1,0:T(8,128)(2,1)S(1)}, bf16[192,192]{1,0:T(8,128)(2,1)}, u32[]{:S(2)}) copy-start(bf16[192,192]{1,0:T(8,128)(2,1)} %constant.113.clone.y_up) | copy-start | bytes 221188

commit v6 on v5

--- a/solution.py
+++ b/solution.py
@@ -54,6 +54,7 @@
     piece = pieces_of(block, flip, place)
     piece, aside = lax.optimization_barrier((piece, aside))
     piece = far_copies(piece, holder // members)
+    piece, aside = lax.optimization_barrier((piece, aside))
     return copies_of(piece, flip).reshape(block.shape), aside
 
 

time: 117 us -> 116 us (level)
  the two profiles are of different devices: /device:TPU:1 before, /device:TPU:129 now
where the time goes in v6:
time: 116 us; the launch traced here: 115 us
  blocking collectives  71.6 us (62%)
  waiting for transfers between devices  26.4 us (23%)
  starting transfers between devices  9.38 us (8%)
  Pallas kernels  6.52 us (6%)
    all_to_all x2, blocking collectives, exchange(): return lax.all_to_all(columns, grid_axes, 0, 0, tiled=True).reshape(shape)  49.6 us
    all_to_all x1, blocking collectives, copies_of(): return lax.all_to_all(copies, axes, 0, 0, tiled=True)  22 us
    all_to_all x1, waiting for transfers between devices, pieces_of(): received = lax.all_to_all(pieces, axes, 0, 0, tiled=True)  14.5 us
    ppermute x3, waiting for transfers between devices, send(): got = lax.ppermute(piece, far_axis, [(first, target)])  11.9 us
    all_to_all x1, starting transfers between devices, pieces_of(): received = lax.all_to_all(pieces, axes, 0, 0, tiled=True)  6.77 us
    pallas_call x3, Pallas kernels, on_device(): pl.pallas_call(body, out_shape=jax.ShapeDtypeStruct(shape, jnp.float32),...  6.52 us
    ppermute x3, starting transfers between devices, send(): got = lax.ppermute(piece, far_axis, [(first, target)])  2.61 us
  transfers between devices with their start and end apart: 4, of which 2 were waited for; matrix products, arithmetic and copies ran while one was open for 0% of the time, Pallas kernels for 0%

profile of v6, /device:TPU:129, one launch (start us, length us, event | category | flops | bytes accessed | tf_op | source)
XLA Modules:
  0.0 115.4 jit_solution(6617309452394518126)
XLA Ops:
  0.0 6.8 %all-to-all-start = ((f32[8,144,128]{2,1,0:T(8,128)}), f32[8,144,128]{2,1,0:T(8,128)S(1)}, u32[]{:S(2)}, u32[]{:S(2)}) async-start(f32[8,144,128]{2,1,0:T(8,128)} %bitcast.20), calls=%async_computation | async-start | bytes 1179648 | tf_op jit(solution)/shard_map/all_to_all | solution.py:22
  7.5 0.0 copy-done.13
  7.5 0.2 copy.16
  7.7 0.1 reshape.26
  7.8 0.1 copy.17
  7.9 14.5 %all-to-all-done = f32[8,144,128]{2,1,0:T(8,128)S(1)} async-done(((f32[8,144,128]{2,1,0:T(8,128)}), f32[8,144,128]{2,1,0:T(8,128)S(1)}, u32[]{:S(2)}, u32[]{:S(2)}) %all-to-all-start) | async-done | bytes 589856 | tf_op jit(solution)/shard_map/all_to_all | solution.py:22
  22.4 14.6 %conditional.1 = (f32[144,128]{1,0:T(8,128)S(1)}) conditional(s32[]{:T(128)} %clamp.3, (s32[]{:T(128)}, f32[144,128]{1,0:T(8,128)S(1)}) %tuple.20, (s32[]{:T(128)}, f32[144,128]{1,0:T(8,128)S(1)}) %tuple.20, (s32[]{:T(128)}, f32[144,128]{1,0:T(8,128)S(1)}) %tuple.20, (s32[]{:T(128)}, f32[144,128]{1,0:T(8,128)S(1)}) %tuple.20), branch_computations={%region_0.1_spmd, %region_1.2_spmd, %region_2.3_spmd, %region_3.4_... | conditional | flops 55299 | bytes 1253534 | solution.py:47
  22.4 0.7 collective-permute-start.11
  23.0 1.3 %collective-permute-start.10 = (f32[144,128]{1,0:T(8,128)S(1)}, f32[144,128]{1,0:T(8,128)S(1)}, u32[]{:S(2)}, u32[]{:S(2)}) collective-permute-start(f32[144,128]{1,0:T(8,128)S(1)} %get-tuple-element.33), channel_id=1, source_target_pairs={{384,128},{385,129},{386,130},{387,131},{388,132},{389,133},{390,1... | collective-permute-start | bytes 221192 | tf_op jit(solution)/shard_map/cond/branch_3_fun/ppermute | solution.py:41
  24.3 0.7 collective-permute-start.9
  25.0 0.0 collective-permute-done.11
  25.0 11.9 %collective-permute-done.10 = f32[144,128]{1,0:T(8,128)S(1)} collective-permute-done((f32[144,128]{1,0:T(8,128)S(1)}, f32[144,128]{1,0:T(8,128)S(1)}, u32[]{:S(2)}, u32[]{:S(2)}) %collective-permute-start.10) | collective-permute-done | bytes 73760 | tf_op jit(solution)/shard_map/cond/branch_3_fun/ppermute | solution.py:41
  36.9 0.0 collective-permute-done.9
  37.0 0.0 copy-start
  37.0 0.0 copy-start.7
  37.0 0.0 copy-start.8
  37.0 0.0 copy-start.11
  37.0 0.0 copy-start.12
  37.1 22.0 %all_to_all.20 = f32[8,144,128]{2,1,0:T(8,128)S(1)} all-to-all(f32[8,144,128]{2,1,0:T(8,128)S(1)} %broadcast_in_dim.2), channel_id=1, replica_groups=mesh['z_far'=4,'z_near'=4,'y_lo'=2,'x'=4,'y_hi'=2,'core'=2] {'y_lo','z_n..., dimensions={0} | all-to-all | bytes 1179648 | tf_op jit(solution)/shard_map/all_to_all | solution.py:28
  59.1 2.2 %shard_map.145 = f32[2304,128]{1,0:T(8,128)S(1)} custom-call(f32[2,6,96,128]{3,2,1,0:T(8,128)S(1)} %copy-done, f32[2,6,96,128]{3,2,1,0:T(8,128)S(1)} %bitcast.21, bf16[256,256]{1,0:T(8,128)(2,1)S(1)} %copy-done.8, bf16[256,256]{1,0:T(8,128)(2,1)S(1)} %copy-done.7, bf16[192,192]{1,0:T(8,128)(2,1)S(1)} %copy-done.12, bf16[192,192]{1,0:T(8,128)(2,1)S(1)} %copy-done.11), custom_call_target="tpu_custom_call" | custom-call | flops 792723456 | bytes 2768896 | tf_op jit(solution)/shard_map/pallas_call | solution.py:194
  61.3 0.0 copy-start.1
  61.4 0.0 copy-start.2
  61.4 0.0 copy-start.3
  61.4 0.0 copy-start.4
  61.4 27.6 %all_to_all.21 = f32[16,144,128]{2,1,0:T(8,128)S(1)} all-to-all(f32[16,144,128]{2,1,0:T(8,128)S(1)} %bitcast.19), channel_id=1, replica_groups=mesh['z_far'=4,'z_near'=4,'y_lo'=2,'x'=4,'y_hi'=2,'core'=2] {'x','y_hi',..., dimensions={0} | all-to-all | bytes 2359296 | tf_op jit(solution)/shard_map/all_to_all | solution.py:225
  89.1 1.8 %shard_map.146 = f32[2304,128]{1,0:T(8,128)S(1)} custom-call(f32[2304,128]{1,0:T(8,128)S(1)} %bitcast.15, f32[96,768]{1,0:T(8,128)S(1)} %bitcast.17, bf16[192,192]{1,0:T(8,128)(2,1)S(1)} %copy-done.4, bf16[192,192]{1,0:T(8,128)(2,1)S(1)} %copy-done.3, bf16[192,192]{1,0:T(8,128)(2,1)S(1)} %copy-done.2, bf16[192,192]{1,0:T(8,128)(2,1)S(1)} %copy-done.1), custom_call_target="tpu_custom_call" | custom-call | flops 679477248 | bytes 2949120 | tf_op jit(solution)/shard_map/pallas_call | solution.py:194
  90.8 0.0 copy-start.5
  90.8 0.0 copy-start.6
  90.8 0.0 copy-start.9
  90.9 0.0 copy-start.10
  90.9 21.9 %all_to_all.22 = f32[16,144,128]{2,1,0:T(8,128)S(1)} all-to-all(f32[16,144,128]{2,1,0:T(8,128)S(1)} %bitcast.16), channel_id=1, replica_groups=mesh['z_far'=4,'z_near'=4,'y_lo'=2,'x'=4,'y_hi'=2,'core'=2] {'x','y_hi',..., dimensions={0} | all-to-all | bytes 2359296 | tf_op jit(solution)/shard_map/all_to_all | solution.py:225
  112.8 2.6 %shard_map.147 = f32[2,6,96,128]{3,2,1,0:T(8,128)} custom-call(f32[2304,128]{1,0:T(8,128)S(1)} %bitcast.18, f32[2,6,96,128]{3,2,1,0:T(8,128)S(1)} %bitcast.22, bf16[192,192]{1,0:T(8,128)(2,1)S(1)} %copy-done.10, bf16[192,192]{1,0:T(8,128)(2,1)S(1)} %copy-done.9, bf16[256,256]{1,0:T(8,128)(2,1)S(1)} %copy-done.6, bf16[256,256]{1,0:T(8,128)(2,1)S(1)} %copy-done.5), custom_call_target="tpu_custom_call" | custom-call | flops 792723456 | bytes 2768896 | tf_op jit(solution)/shard_map/pallas_call | solution.py:194
  (17 shorter events, 0.1 us)
Async XLA Ops:
  0.0 7.5 %copy-start.13 = (f32[96,6,128]{2,0,1:T(8,128)S(1)}, f32[96,6,128]{2,0,1:T(8,128)}, u32[]{:S(2)}) copy-start(f32[96,6,128]{2,0,1:T(8,128)} %param.20) | copy-start | bytes 884740
  0.0 22.4 %all-to-all-start = ((f32[8,144,128]{2,1,0:T(8,128)}), f32[8,144,128]{2,1,0:T(8,128)S(1)}, u32[]{:S(2)}, u32[]{:S(2)}) async-start(f32[8,144,128]{2,1,0:T(8,128)} %bitcast.20), calls=%async_computation | async-start | bytes 1179648 | tf_op jit(solution)/shard_map/all_to_all | solution.py:22
  22.4 2.6 %collective-permute-start.11 = (f32[144,128]{1,0:T(8,128)S(1)}, f32[144,128]{1,0:T(8,128)S(1)}, u32[]{:S(2)}, u32[]{:S(2)}) collective-permute-start(f32[144,128]{1,0:T(8,128)S(1)} %get-tuple-element.33), channel_id=1, source_target_pairs={{384,0},{385,1},{386,2},{387,3},{388,4},{389,5},{390,6},{391,7},{3... | collective-permute-start | bytes 221192 | tf_op jit(solution)/shard_map/cond/branch_3_fun/ppermute | solution.py:41
  23.0 13.9 %collective-permute-start.10 = (f32[144,128]{1,0:T(8,128)S(1)}, f32[144,128]{1,0:T(8,128)S(1)}, u32[]{:S(2)}, u32[]{:S(2)}) collective-permute-start(f32[144,128]{1,0:T(8,128)S(1)} %get-tuple-element.33), channel_id=1, source_target_pairs={{384,128},{385,129},{386,130},{387,131},{388,132},{389,133},{390,1... | collective-permute-start | bytes 221192 | tf_op jit(solution)/shard_map/cond/branch_3_fun/ppermute | solution.py:41
  24.3 12.6 %collective-permute-start.9 = (f32[144,128]{1,0:T(8,128)S(1)}, f32[144,128]{1,0:T(8,128)S(1)}, u32[]{:S(2)}, u32[]{:S(2)}) collective-permute-start(f32[144,128]{1,0:T(8,128)S(1)} %get-tuple-element.33), channel_id=1, source_target_pairs={{384,256},{385,257},{386,258},{387,259},{388,260},{389,261},{390,2... | collective-permute-start | bytes 221192 | tf_op jit(solution)/shard_map/cond/branch_3_fun/ppermute | solution.py:41
  37.0 22.1 %copy-start = (f32[2,6,96,128]{3,2,1,0:T(8,128)S(1)}, f32[2,6,96,128]{3,2,1,0:T(8,128)}, u32[]{:S(2)}) copy-start(f32[2,6,96,128]{3,2,1,0:T(8,128)} %orbitals.1) | copy-start | bytes 1769476
  37.0 22.1 %copy-start.7 = (bf16[256,256]{1,0:T(8,128)(2,1)S(1)}, bf16[256,256]{1,0:T(8,128)(2,1)}, u32[]{:S(2)}) copy-start(bf16[256,256]{1,0:T(8,128)(2,1)} %constant.106.clone.z_low) | copy-start | bytes 393220
  37.0 22.1 %copy-start.8 = (bf16[256,256]{1,0:T(8,128)(2,1)S(1)}, bf16[256,256]{1,0:T(8,128)(2,1)}, u32[]{:S(2)}) copy-start(bf16[256,256]{1,0:T(8,128)(2,1)} %constant.105.clone.z_up) | copy-start | bytes 393220
  37.0 22.1 %copy-start.11 = (bf16[192,192]{1,0:T(8,128)(2,1)S(1)}, bf16[192,192]{1,0:T(8,128)(2,1)}, u32[]{:S(2)}) copy-start(bf16[192,192]{1,0:T(8,128)(2,1)} %constant.108.clone.y_low) | copy-start | bytes 221188
  37.0 22.1 %copy-start.12 = (bf16[192,192]{1,0:T(8,128)(2,1)S(1)}, bf16[192,192]{1,0:T(8,128)(2,1)}, u32[]{:S(2)}) copy-start(bf16[192,192]{1,0:T(8,128)(2,1)} %constant.107.clone.y_up) | copy-start | bytes 221188
  61.3 27.7 %copy-start.1 = (bf16[192,192]{1,0:T(8,128)(2,1)S(1)}, bf16[192,192]{1,0:T(8,128)(2,1)}, u32[]{:S(2)}) copy-start(bf16[192,192]{1,0:T(8,128)(2,1)} %constant.112.clone.i_low) | copy-start | bytes 221188
  61.4 27.7 %copy-start.2 = (bf16[192,192]{1,0:T(8,128)(2,1)S(1)}, bf16[192,192]{1,0:T(8,128)(2,1)}, u32[]{:S(2)}) copy-start(bf16[192,192]{1,0:T(8,128)(2,1)} %constant.111.clone.i_up) | copy-start | bytes 221188
  61.4 27.7 %copy-start.3 = (bf16[192,192]{1,0:T(8,128)(2,1)S(1)}, bf16[192,192]{1,0:T(8,128)(2,1)}, u32[]{:S(2)}) copy-start(bf16[192,192]{1,0:T(8,128)(2,1)} %constant.110.clone.f_low) | copy-start | bytes 221188
  61.4 27.7 %copy-start.4 = (bf16[192,192]{1,0:T(8,128)(2,1)S(1)}, bf16[192,192]{1,0:T(8,128)(2,1)}, u32[]{:S(2)}) copy-start(bf16[192,192]{1,0:T(8,128)(2,1)} %constant.109.clone.f_up) | copy-start | bytes 221188
  90.8 22.0 %copy-start.5 = (bf16[256,256]{1,0:T(8,128)(2,1)S(1)}, bf16[256,256]{1,0:T(8,128)(2,1)}, u32[]{:S(2)}) copy-start(bf16[256,256]{1,0:T(8,128)(2,1)} %constant.116.clone.z_low) | copy-start | bytes 393220
  90.8 22.0 %copy-start.6 = (bf16[256,256]{1,0:T(8,128)(2,1)S(1)}, bf16[256,256]{1,0:T(8,128)(2,1)}, u32[]{:S(2)}) copy-start(bf16[256,256]{1,0:T(8,128)(2,1)} %constant.115.clone.z_up) | copy-start | bytes 393220
  90.8 22.0 %copy-start.9 = (bf16[192,192]{1,0:T(8,128)(2,1)S(1)}, bf16[192,192]{1,0:T(8,128)(2,1)}, u32[]{:S(2)}) copy-start(bf16[192,192]{1,0:T(8,128)(2,1)} %constant.114.clone.y_low) | copy-start | bytes 221188
  90.9 22.0 %copy-start.10 = (bf16[192,192]{1,0:T(8,128)(2,1)S(1)}, bf16[192,192]{1,0:T(8,128)(2,1)}, u32[]{:S(2)}) copy-start(bf16[192,192]{1,0:T(8,128)(2,1)} %constant.113.clone.y_up) | copy-start | bytes 221188

commit v7 on v6

--- a/solution.py
+++ b/solution.py
@@ -51,7 +51,13 @@
     members = lax.axis_size(near_axes)
     flip = near_axes[::-1]
     place = (holder % 2) * (members // 2) + (holder % members) // 2
-    piece = pieces_of(block, flip, place)
+    source = holder // members
+    piece = lax.cond(
+        (source > 0) | (lax.axis_index(far_axis) == source),
+        lambda block: pieces_of(block, flip, place),
+        lambda block: jnp.zeros((block.size // (members * lanes), lanes), block.dtype),
+        block,
+    )
     piece, aside = lax.optimization_barrier((piece, aside))
     piece = far_copies(piece, holder // members)
     piece, aside = lax.optimization_barrier((piece, aside))

time: 116 us -> 117 us (level)
  no operation moved by 1% of the time
where the time goes in v7:
time: 117 us
  blocking collectives  71.6 us (61%)
  waiting for transfers between devices  27.3 us (23%)
  starting transfers between devices  9.26 us (8%)
  Pallas kernels  6.51 us (6%)
  local copies, waits for them, and re-layouts  1.44 us (1%)
    all_to_all x2, blocking collectives, exchange(): return lax.all_to_all(columns, grid_axes, 0, 0, tiled=True).reshape(shape)  49.6 us
    all_to_all x1, blocking collectives, copies_of(): return lax.all_to_all(copies, axes, 0, 0, tiled=True)  22 us
    all_to_all x1, waiting for transfers between devices, pieces_of(): received = lax.all_to_all(pieces, axes, 0, 0, tiled=True)  15.4 us
    ppermute x3, waiting for transfers between devices, send(): got = lax.ppermute(piece, far_axis, [(first, target)])  11.9 us
    all_to_all x1, starting transfers between devices, pieces_of(): received = lax.all_to_all(pieces, axes, 0, 0, tiled=True)  6.65 us
    pallas_call x3, Pallas kernels, on_device(): pl.pallas_call(body, out_shape=jax.ShapeDtypeStruct(shape, jnp.float32),...  6.51 us
    ppermute x3, starting transfers between devices, send(): got = lax.ppermute(piece, far_axis, [(first, target)])  2.62 us
  transfers between devices with their start and end apart: 4, of which 2 were waited for; matrix products, arithmetic and copies ran while one was open for 0% of the time, Pallas kernels for 0%

profile of v7, /device:TPU:129, one launch (start us, length us, event | category | flops | bytes accessed | tf_op | source)
XLA Modules:
  0.0 117.2 jit_solution(13840283330169536334)
XLA Ops:
  0.8 1.1 copy.16
  1.9 0.1 reshape.25
  2.0 0.1 copy.17
  2.1 22.1 %conditional.2 = (f32[144,128]{1,0:T(8,128)S(1)}) conditional(s32[]{:T(128)} %convert_element_type.3, () %tuple.25, (f32[2,6,96,128]{3,2,1,0:T(8,128)S(1)}, s32[]{:T(128)}, s32[]{:T(128)}, (), s32[]{:T(128)}, /*index=5*/s32[]{:T(128)}, s32[]{:T(128)}, s32[]{:T(128)}, pred[]{:T(512)}, s32[]{:T(128)}, /*index=10*/s32[]{:T(128)}, (), s32[]{:T(128)}, ...), branch_computations={%region_0.1_spmd, %region_1.2_spmd} | conditional | flops 18 | bytes 1917151 | solution.py:55
  2.1 6.6 %all-to-all-start = ((f32[8,144,128]{2,1,0:T(8,128)S(1)}), f32[8,144,128]{2,1,0:T(8,128)S(1)}, u32[]{:S(2)}, u32[]{:S(2)}) async-start(f32[8,144,128]{2,1,0:T(8,128)S(1)} %bitcast.23), calls=%async_computation | async-start | bytes 1179648 | tf_op jit(solution)/shard_map/cond/branch_1_fun/all_to_all | solution.py:22
  8.8 15.4 %all-to-all-done = f32[8,144,128]{2,1,0:T(8,128)S(1)} async-done(((f32[8,144,128]{2,1,0:T(8,128)S(1)}), f32[8,144,128]{2,1,0:T(8,128)S(1)}, u32[]{:S(2)}, u32[]{:S(2)}) %all-to-all-start) | async-done | bytes 589856 | tf_op jit(solution)/shard_map/cond/branch_1_fun/all_to_all | solution.py:22
  24.2 14.6 %conditional.3 = (f32[144,128]{1,0:T(8,128)S(1)}) conditional(s32[]{:T(128)} %clamp.3, (s32[]{:T(128)}, f32[144,128]{1,0:T(8,128)S(1)}) %tuple.28, (s32[]{:T(128)}, f32[144,128]{1,0:T(8,128)S(1)}) %tuple.28, (s32[]{:T(128)}, f32[144,128]{1,0:T(8,128)S(1)}) %tuple.28, (s32[]{:T(128)}, f32[144,128]{1,0:T(8,128)S(1)}) %tuple.28), branch_computations={%region_2.3_spmd, %region_3.4_spmd, %region_4.5_spmd, %region_5.6_... | conditional | flops 55299 | bytes 1253534 | solution.py:47
  24.2 0.7 collective-permute-start.11
  24.8 1.3 %collective-permute-start.10 = (f32[144,128]{1,0:T(8,128)S(1)}, f32[144,128]{1,0:T(8,128)S(1)}, u32[]{:S(2)}, u32[]{:S(2)}) collective-permute-start(f32[144,128]{1,0:T(8,128)S(1)} %get-tuple-element.42), channel_id=1, source_target_pairs={{384,128},{385,129},{386,130},{387,131},{388,132},{389,133},{390,1... | collective-permute-start | bytes 221192 | tf_op jit(solution)/shard_map/cond/branch_3_fun/ppermute | solution.py:41
  26.1 0.7 collective-permute-start.9
  26.8 0.0 collective-permute-done.11
  26.8 11.9 %collective-permute-done.10 = f32[144,128]{1,0:T(8,128)S(1)} collective-permute-done((f32[144,128]{1,0:T(8,128)S(1)}, f32[144,128]{1,0:T(8,128)S(1)}, u32[]{:S(2)}, u32[]{:S(2)}) %collective-permute-start.10) | collective-permute-done | bytes 73760 | tf_op jit(solution)/shard_map/cond/branch_3_fun/ppermute | solution.py:41
  38.7 0.0 collective-permute-done.9
  38.8 0.0 copy-start.6
  38.8 0.0 copy-start.7
  38.8 0.0 copy-start.10
  38.8 0.0 copy-start.11
  38.9 22.0 %all_to_all.19 = f32[8,144,128]{2,1,0:T(8,128)S(1)} all-to-all(f32[8,144,128]{2,1,0:T(8,128)S(1)} %broadcast_in_dim.2), channel_id=1, replica_groups=mesh['z_far'=4,'z_near'=4,'y_lo'=2,'x'=4,'y_hi'=2,'core'=2] {'y_lo','z_n..., dimensions={0} | all-to-all | bytes 1179648 | tf_op jit(solution)/shard_map/all_to_all | solution.py:28
  60.9 0.0 copy-done.10
  60.9 2.2 %shard_map.145 = f32[2304,128]{1,0:T(8,128)S(1)} custom-call(f32[2,6,96,128]{3,2,1,0:T(8,128)S(1)} %copy-done.12, f32[2,6,96,128]{3,2,1,0:T(8,128)S(1)} %bitcast.20, bf16[256,256]{1,0:T(8,128)(2,1)S(1)} %copy-done.7, bf16[256,256]{1,0:T(8,128)(2,1)S(1)} %copy-done.6, bf16[192,192]{1,0:T(8,128)(2,1)S(1)} %copy-done.11, bf16[192,192]{1,0:T(8,128)(2,1)S(1)} %copy-done.10), custom_call_target="tpu_custom_call" | custom-call | flops 792723456 | bytes 2768896 | tf_op jit(solution)/shard_map/pallas_call | solution.py:200
  63.1 0.0 copy-start
  63.1 0.0 copy-start.1
  63.1 0.0 copy-start.2
  63.2 0.0 copy-start.3
  63.2 27.6 %all_to_all.20 = f32[16,144,128]{2,1,0:T(8,128)S(1)} all-to-all(f32[16,144,128]{2,1,0:T(8,128)S(1)} %bitcast.19), channel_id=1, replica_groups=mesh['z_far'=4,'z_near'=4,'y_lo'=2,'x'=4,'y_hi'=2,'core'=2] {'x','y_hi',..., dimensions={0} | all-to-all | bytes 2359296 | tf_op jit(solution)/shard_map/all_to_all | solution.py:231
  90.8 1.8 %shard_map.146 = f32[2304,128]{1,0:T(8,128)S(1)} custom-call(f32[2304,128]{1,0:T(8,128)S(1)} %bitcast.15, f32[96,768]{1,0:T(8,128)S(1)} %bitcast.17, bf16[192,192]{1,0:T(8,128)(2,1)S(1)} %copy-done.3, bf16[192,192]{1,0:T(8,128)(2,1)S(1)} %copy-done.2, bf16[192,192]{1,0:T(8,128)(2,1)S(1)} %copy-done.1, bf16[192,192]{1,0:T(8,128)(2,1)S(1)} %copy-done), custom_call_target="tpu_custom_call" | custom-call | flops 679477248 | bytes 2949120 | tf_op jit(solution)/shard_map/pallas_call | solution.py:200
  92.6 0.0 copy-start.4
  92.6 0.0 copy-start.5
  92.6 0.0 copy-start.8
  92.6 0.0 copy-start.9
  92.6 21.9 %all_to_all.21 = f32[16,144,128]{2,1,0:T(8,128)S(1)} all-to-all(f32[16,144,128]{2,1,0:T(8,128)S(1)} %bitcast.16), channel_id=1, replica_groups=mesh['z_far'=4,'z_near'=4,'y_lo'=2,'x'=4,'y_hi'=2,'core'=2] {'x','y_hi',..., dimensions={0} | all-to-all | bytes 2359296 | tf_op jit(solution)/shard_map/all_to_all | solution.py:231
  114.6 2.5 %shard_map.147 = f32[2,6,96,128]{3,2,1,0:T(8,128)} custom-call(f32[2304,128]{1,0:T(8,128)S(1)} %bitcast.18, f32[2,6,96,128]{3,2,1,0:T(8,128)S(1)} %bitcast.21, bf16[192,192]{1,0:T(8,128)(2,1)S(1)} %copy-done.9, bf16[192,192]{1,0:T(8,128)(2,1)S(1)} %copy-done.8, bf16[256,256]{1,0:T(8,128)(2,1)S(1)} %copy-done.5, bf16[256,256]{1,0:T(8,128)(2,1)S(1)} %copy-done.4), custom_call_target="tpu_custom_call" | custom-call | flops 792723456 | bytes 2768896 | tf_op jit(solution)/shard_map/pallas_call | solution.py:200
  (16 shorter events, 0.1 us)
Async XLA Ops:
  0.0 2.1 %copy-start.12 = (f32[2,6,96,128]{3,2,1,0:T(8,128)S(1)}, f32[2,6,96,128]{3,2,1,0:T(8,128)}, u32[]{:S(2)}) copy-start(f32[2,6,96,128]{3,2,1,0:T(8,128)} %orbitals.1) | copy-start | bytes 1769476
  2.1 22.0 %all-to-all-start = ((f32[8,144,128]{2,1,0:T(8,128)S(1)}), f32[8,144,128]{2,1,0:T(8,128)S(1)}, u32[]{:S(2)}, u32[]{:S(2)}) async-start(f32[8,144,128]{2,1,0:T(8,128)S(1)} %bitcast.23), calls=%async_computation | async-start | bytes 1179648 | tf_op jit(solution)/shard_map/cond/branch_1_fun/all_to_all | solution.py:22
  24.2 2.7 %collective-permute-start.11 = (f32[144,128]{1,0:T(8,128)S(1)}, f32[144,128]{1,0:T(8,128)S(1)}, u32[]{:S(2)}, u32[]{:S(2)}) collective-permute-start(f32[144,128]{1,0:T(8,128)S(1)} %get-tuple-element.42), channel_id=1, source_target_pairs={{384,0},{385,1},{386,2},{387,3},{388,4},{389,5},{390,6},{391,7},{3... | collective-permute-start | bytes 221192 | tf_op jit(solution)/shard_map/cond/branch_3_fun/ppermute | solution.py:41
  24.8 13.9 %collective-permute-start.10 = (f32[144,128]{1,0:T(8,128)S(1)}, f32[144,128]{1,0:T(8,128)S(1)}, u32[]{:S(2)}, u32[]{:S(2)}) collective-permute-start(f32[144,128]{1,0:T(8,128)S(1)} %get-tuple-element.42), channel_id=1, source_target_pairs={{384,128},{385,129},{386,130},{387,131},{388,132},{389,133},{390,1... | collective-permute-start | bytes 221192 | tf_op jit(solution)/shard_map/cond/branch_3_fun/ppermute | solution.py:41
  26.1 12.6 %collective-permute-start.9 = (f32[144,128]{1,0:T(8,128)S(1)}, f32[144,128]{1,0:T(8,128)S(1)}, u32[]{:S(2)}, u32[]{:S(2)}) collective-permute-start(f32[144,128]{1,0:T(8,128)S(1)} %get-tuple-element.42), channel_id=1, source_target_pairs={{384,256},{385,257},{386,258},{387,259},{388,260},{389,261},{390,2... | collective-permute-start | bytes 221192 | tf_op jit(solution)/shard_map/cond/branch_3_fun/ppermute | solution.py:41
  38.8 22.1 %copy-start.6 = (bf16[256,256]{1,0:T(8,128)(2,1)S(1)}, bf16[256,256]{1,0:T(8,128)(2,1)}, u32[]{:S(2)}) copy-start(bf16[256,256]{1,0:T(8,128)(2,1)} %constant.112.clone.z_low) | copy-start | bytes 393220
  38.8 22.1 %copy-start.7 = (bf16[256,256]{1,0:T(8,128)(2,1)S(1)}, bf16[256,256]{1,0:T(8,128)(2,1)}, u32[]{:S(2)}) copy-start(bf16[256,256]{1,0:T(8,128)(2,1)} %constant.111.clone.z_up) | copy-start | bytes 393220
  38.8 22.1 %copy-start.10 = (bf16[192,192]{1,0:T(8,128)(2,1)S(1)}, bf16[192,192]{1,0:T(8,128)(2,1)}, u32[]{:S(2)}) copy-start(bf16[192,192]{1,0:T(8,128)(2,1)} %constant.114.clone.y_low) | copy-start | bytes 221188
  38.8 22.1 %copy-start.11 = (bf16[192,192]{1,0:T(8,128)(2,1)S(1)}, bf16[192,192]{1,0:T(8,128)(2,1)}, u32[]{:S(2)}) copy-start(bf16[192,192]{1,0:T(8,128)(2,1)} %constant.113.clone.y_up) | copy-start | bytes 221188
  63.1 27.7 %copy-start = (bf16[192,192]{1,0:T(8,128)(2,1)S(1)}, bf16[192,192]{1,0:T(8,128)(2,1)}, u32[]{:S(2)}) copy-start(bf16[192,192]{1,0:T(8,128)(2,1)} %constant.118.clone.i_low) | copy-start | bytes 221188
  63.1 27.7 %copy-start.1 = (bf16[192,192]{1,0:T(8,128)(2,1)S(1)}, bf16[192,192]{1,0:T(8,128)(2,1)}, u32[]{:S(2)}) copy-start(bf16[192,192]{1,0:T(8,128)(2,1)} %constant.117.clone.i_up) | copy-start | bytes 221188
  63.1 27.7 %copy-start.2 = (bf16[192,192]{1,0:T(8,128)(2,1)S(1)}, bf16[192,192]{1,0:T(8,128)(2,1)}, u32[]{:S(2)}) copy-start(bf16[192,192]{1,0:T(8,128)(2,1)} %constant.116.clone.f_low) | copy-start | bytes 221188
  63.2 27.7 %copy-start.3 = (bf16[192,192]{1,0:T(8,128)(2,1)S(1)}, bf16[192,192]{1,0:T(8,128)(2,1)}, u32[]{:S(2)}) copy-start(bf16[192,192]{1,0:T(8,128)(2,1)} %constant.115.clone.f_up) | copy-start | bytes 221188
  92.6 22.0 %copy-start.4 = (bf16[256,256]{1,0:T(8,128)(2,1)S(1)}, bf16[256,256]{1,0:T(8,128)(2,1)}, u32[]{:S(2)}) copy-start(bf16[256,256]{1,0:T(8,128)(2,1)} %constant.122.clone.z_low) | copy-start | bytes 393220
  92.6 22.0 %copy-start.5 = (bf16[256,256]{1,0:T(8,128)(2,1)S(1)}, bf16[256,256]{1,0:T(8,128)(2,1)}, u32[]{:S(2)}) copy-start(bf16[256,256]{1,0:T(8,128)(2,1)} %constant.121.clone.z_up) | copy-start | bytes 393220
  92.6 22.0 %copy-start.8 = (bf16[192,192]{1,0:T(8,128)(2,1)S(1)}, bf16[192,192]{1,0:T(8,128)(2,1)}, u32[]{:S(2)}) copy-start(bf16[192,192]{1,0:T(8,128)(2,1)} %constant.120.clone.y_low) | copy-start | bytes 221188
  92.6 22.0 %copy-start.9 = (bf16[192,192]{1,0:T(8,128)(2,1)S(1)}, bf16[192,192]{1,0:T(8,128)(2,1)}, u32[]{:S(2)}) copy-start(bf16[192,192]{1,0:T(8,128)(2,1)} %constant.119.clone.y_up) | copy-start | bytes 221188
